TPU v7x, 512 devices: a whole 4x8x8 slice. The times are simulated.
512 devices in a mesh: seq: 128 (over x_hi, z, y), tp: 4 (over x_lo, core).
Axes of the slice: x: 4 (x_hi: 2, x_lo: 2; x = x_hi * 2 + x_lo), y: 8, z: 8, core: 2. Of those that a mesh axis runs over, the one named last changes fastest.
Arguments:
- frames: bfloat16 [6144, 1024], P('seq'), may hold values from -6 to 6
- query_rows: bfloat16 [6144, 1024], P('seq', 'tp'), may hold values from -6 to 6
- key_rows: bfloat16 [6144, 1024], P('seq', 'tp'), may hold values from -6 to 6
- value_rows: bfloat16 [6144, 1024], P('seq', 'tp'), may hold values from -48 to 48
- w_out: bfloat16 [1024, 1024], P('tp'), may hold values from -0.1875 to 0.1875
- w_in: bfloat16 [1024, 2, 2048], P(None, None, 'tp'), may hold values from -0.84375 to 0.84375
- w_conv: float32 [31, 2048], P(None, 'tp'), may hold values from -1 to 1
- w_proj: bfloat16 [2048, 1024], P('tp'), may hold values from -0.125 to 0.125
- w_blend: float32 [31, 2, 1024], P(None, None, 'tp'), may hold values from -1 to 1
- w_merge: bfloat16 [2, 1024, 1024], P(None, 'tp'), may hold values from -0.125 to 0.125
Outputs:
- merged: bfloat16 [6144, 1024], P('seq', 'tp')
All inputs are finite; a program needn't handle non-finite values.
Results may differ from a plain program's by a relative error of at most 0.023.
Values may be sent and summed in bfloat16 or wider, within the bound.
A program may use at most 64 MiB of HBM per device.

v0:
```python
import jax
import jax.numpy as jnp
from jax import lax
from jax.sharding import PartitionSpec as P

HEAD = 64
KCONV = 31
KMERGE = 31
CH = 2048


def with_halo(cells, sides, width):
    for axis, dim in sides:
        count = lax.axis_size(axis)
        ends = count - 1
        head = lax.slice_in_dim(cells, 0, width, axis=dim)
        tail = lax.slice_in_dim(cells, cells.shape[dim] - width, cells.shape[dim], axis=dim)
        cells = jnp.concatenate(
            [
                lax.ppermute(tail, axis, [(i, (i + 1) % count) for i in range(ends)]),
                cells,
                lax.ppermute(head, axis, [((i + 1) % count, i) for i in range(ends)]),
            ],
            axis=dim,
        )
    return cells


def normalize_rows(features):
    average = jnp.mean(features, -1, keepdims=True)
    centered = features - average
    variance = jnp.mean(centered * centered, -1, keepdims=True)
    return centered * lax.rsqrt(variance + 1e-05)


def depthwise(padded, tap_weights, row_count):
    result = jnp.zeros((row_count, padded.shape[1]), jnp.float32)
    for offset in range(tap_weights.shape[0]):
        result = result + tap_weights[offset] * padded[offset : offset + row_count].astype(
            jnp.float32
        )
    return result


def normalize_gate(gate_float, sum_rows, sum_squares):
    average = sum_rows / CH
    variance = sum_squares / CH - average * average
    return ((gate_float - average[:, None]) * lax.rsqrt(variance + 1e-05)[:, None]).astype(
        jnp.bfloat16
    )


def on_device(
    frames, query_rows, key_rows, value_rows, w_out, w_in, w_conv, w_proj, w_blend, w_merge
):
    row_count = query_rows.shape[0]
    head_count = query_rows.shape[1] // HEAD
    key_whole, value_whole = (
        lax.all_gather(key_rows, "seq", axis=0, tiled=True),
        lax.all_gather(value_rows, "seq", axis=0, tiled=True),
    )
    head_outputs = []
    for head_index in range(head_count):
        head_start = head_index * HEAD
        scores = jnp.einsum(
            "qd,kd->qk",
            query_rows[:, head_start : head_start + HEAD],
            key_whole[:, head_start : head_start + HEAD],
            preferred_element_type=jnp.float32,
        ) * HEAD ** (-0.5)
        peak_score = jnp.max(scores, -1, keepdims=True)
        exp_scores = jnp.exp(scores - peak_score)
        prob_total = jnp.sum(exp_scores, -1, keepdims=True)
        weights = exp_scores.astype(jnp.bfloat16)
        head_value = jnp.dot(
            weights,
            value_whole[:, head_start : head_start + HEAD],
            preferred_element_type=jnp.float32,
        )
        head_outputs.append((head_value / prob_total).astype(jnp.bfloat16))
    attended = jnp.concatenate(head_outputs, axis=1)
    att_part = jnp.dot(attended, w_out, preferred_element_type=jnp.float32)
    normed = normalize_rows(frames.astype(jnp.float32)).astype(jnp.bfloat16)
    local_units = w_in.shape[2]
    hidden = jax.nn.gelu(
        jnp.dot(
            normed, w_in.reshape(w_in.shape[0], 2 * local_units), preferred_element_type=jnp.float32
        ),
        approximate=False,
    ).astype(jnp.bfloat16)
    resid_half = hidden[:, :local_units]
    gate_half = hidden[:, local_units:]
    halo_reach = (KCONV - 1) // 2
    gate_float = gate_half.astype(jnp.float32)
    sum_rows, sum_squares = lax.psum(
        (jnp.sum(gate_float, -1), jnp.sum(gate_float * gate_float, -1)), "tp"
    )
    gate_norm = normalize_gate(gate_float, sum_rows, sum_squares)
    gate_padded = with_halo(gate_norm, (("seq", 0),), halo_reach)
    conv_out = depthwise(gate_padded, w_conv, row_count)
    gated_rows = (resid_half.astype(jnp.float32) * conv_out).astype(jnp.bfloat16)
    cg_part = jnp.dot(gated_rows, w_proj, preferred_element_type=jnp.float32)
    att_out, cg_out = (
        lax.psum_scatter(
            att_part.astype(jnp.bfloat16), "tp", scatter_dimension=1, tiled=True
        ).astype(jnp.float32),
        lax.psum_scatter(
            cg_part.astype(jnp.bfloat16), "tp", scatter_dimension=1, tiled=True
        ).astype(jnp.float32),
    )
    joined = jnp.concatenate([att_out.astype(jnp.bfloat16), cg_out.astype(jnp.bfloat16)], axis=1)
    merge_reach = (KMERGE - 1) // 2
    joined_wide = with_halo(joined, (("seq", 0),), merge_reach)
    blend_taps = w_blend.reshape(w_blend.shape[0], joined.shape[1])
    mixture = (joined.astype(jnp.float32) + depthwise(joined_wide, blend_taps, row_count)).astype(
        jnp.bfloat16
    )
    merge_part = jnp.dot(
        mixture,
        w_merge.reshape(joined.shape[1], w_merge.shape[2]),
        preferred_element_type=jnp.float32,
    )
    merged_part = lax.psum_scatter(
        merge_part.astype(jnp.bfloat16), "tp", scatter_dimension=1, tiled=True
    ).astype(jnp.float32)
    local_width = merged_part.shape[1]
    residual = lax.dynamic_slice_in_dim(frames, lax.axis_index("tp") * local_width, local_width, 1)
    return (residual.astype(jnp.float32) + merged_part).astype(jnp.bfloat16)


def solution(mesh):
    return jax.shard_map(
        on_device,
        mesh=mesh,
        in_specs=(
            P("seq", None),
            P("seq", "tp"),
            P("seq", "tp"),
            P("seq", "tp"),
            P("tp", None),
            P(None, None, "tp"),
            P(None, "tp"),
            P("tp", None),
            P(None, None, "tp"),
            P(None, "tp", None),
        ),
        out_specs=P("seq", "tp"),
        check_vma=False,
    )
```

profile of v0, /device:TPU:1, one launch (start us, length us, event | category | flops | bytes accessed | tf_op | source)
XLA Modules:
  0.0 377.1 jit_solution(16395602057736794978)
XLA Ops:
  6.5 0.7 all-gather.3.cloned.1.call-update
  7.3 0.0 all-gather.5.cloned.1.call-start
  7.3 0.7 all-gather.5.cloned.1.call-update
  8.0 0.0 reduce-scatter.4.cloned.1.call-start
  8.1 0.0 copy-start.8
  8.1 2.2 copy.11
  10.3 0.1 convert_reduce_fusion
  10.4 0.2 fusion.54
  10.6 0.0 copy-start.14
  10.6 0.0 copy-start.9
  10.6 0.9 fusion.58
  11.5 0.1 convert_reduce_fusion.1
  11.7 11.9 %all-reduce = (f32[48]{0:T(128)S(1)}, f32[48]{0:T(128)S(1)}) all-reduce(f32[48]{0:T(128)S(1)} %get-tuple-element.6, f32[48]{0:T(128)S(1)} %get-tuple-element.5), channel_id=1, replica_groups=mesh['seq'=128,'tp'=4] {'tp'}, use_global_device_ids=true, to_apply=%region_14.0 | all-reduce | flops 96 | bytes 768 | tf_op jit(solution)/shard_map/psum | solution.py:95
  23.6 0.1 fusion.83
  23.7 0.6 fusion.166
  24.3 1.3 collective-permute-start.1
  25.6 4.6 %collective-permute-start = (bf16[15,512]{1,0:T(8,128)(2,1)}, bf16[15,512]{1,0:T(8,128)(2,1)}, u32[]{:S(2)}, u32[]{:S(2)}) collective-permute-start(bf16[15,512]{1,0:T(8,128)(2,1)} %get-tuple-element.73), channel_id=1, source_target_pairs={{0,4},{4,8},{8,12},{12,16},{16,20},{20,24},{24,28},{28,32},{32,36}... | collective-permute-start | bytes 46088 | tf_op jit(solution)/shard_map/ppermute | solution.py:20
  30.2 0.7 fusion.164
  30.8 0.7 fusion.163
  31.5 115.2 %all-gather.3.cloned.1.call-done = bf16[6144,256]{1,0:T(8,128)(2,1)} async-done(((bf16[48,256]{1,0:T(8,128)(2,1)}), bf16[6144,256]{1,0:T(8,128)(2,1)}) %all-gather.3.cloned.1.call-update) | async-done | bytes 3145744 | tf_op jit(solution)/shard_map/all_gather | solution.py:59
  146.7 2.3 fusion.167
  149.0 0.0 copy-start.10
  149.0 0.6 copy-done.15
  149.6 0.9 fusion.42
  150.5 0.0 copy-done.2
  150.5 0.7 fusion.168
  151.3 0.5 copy-done.16
  151.8 0.8 fusion.40
  152.6 0.8 fusion.169
  153.4 0.5 copy-done.17
  153.9 0.9 fusion.38
  154.9 0.7 fusion.170
  155.6 1.0 copy-done.5
  156.7 0.9 fusion.36
  157.5 121.8 %all-gather.5.cloned.1.call-done = bf16[6144,256]{1,0:T(8,128)(2,1)} async-done(((bf16[48,256]{1,0:T(8,128)(2,1)}), bf16[6144,256]{1,0:T(8,128)(2,1)}) %all-gather.5.cloned.1.call-update) | async-done | bytes 3145744 | tf_op jit(solution)/shard_map/all_gather | solution.py:60
  279.3 2.3 fusion.24
  281.7 1.9 fusion.27
  283.6 0.0 copy-done.1
  283.6 0.0 copy-done.4
  283.7 0.7 fusion.30
  284.4 0.5 copy-done.6
  285.2 0.4 fusion.33
  285.7 0.3 copy-done.7
  286.0 0.9 convolution_convert_fusion.2
  286.9 0.0 reduce-scatter.4.cloned.1.call-update
  286.9 0.0 reduce-scatter.6.cloned.1.call-start
  286.9 0.0 collective-permute-done.1
  286.9 0.0 collective-permute-done
  287.3 0.0 copy-start.13
  287.3 3.3 convolution_convert_fusion.1
  290.6 0.0 reduce-scatter.6.cloned.1.call-update
  290.6 0.0 reduce-scatter.8.cloned.1.call-start
  290.7 17.8 %reduce-scatter.4.cloned.1.call-done = bf16[48,256]{1,0:T(8,128)(2,1)} async-done(((bf16[48,1024]{1,0:T(8,128)(2,1)}), bf16[48,256]{1,0:T(8,128)(2,1)}) %reduce-scatter.4.cloned.1.call-update) | async-done | bytes 24592 | tf_op jit(solution)/shard_map/reduce_scatter | solution.py:104
  308.5 0.7 constant_dynamic-update-slice_fusion.1
  309.2 25.3 %reduce-scatter.6.cloned.1.call-done = bf16[48,256]{1,0:T(8,128)(2,1)} async-done(((bf16[48,1024]{1,0:T(8,128)(2,1)}), bf16[48,256]{1,0:T(8,128)(2,1)}) %reduce-scatter.6.cloned.1.call-update) | async-done | bytes 24592 | tf_op jit(solution)/shard_map/reduce_scatter | solution.py:107
  334.5 0.7 constant_dynamic-update-slice_fusion
  335.2 1.3 collective-permute-start.3
  336.5 4.0 %collective-permute-start.2 = (bf16[15,512]{1,0:T(8,128)(2,1)S(1)}, bf16[15,512]{1,0:T(8,128)(2,1)S(1)}, u32[]{:S(2)}, u32[]{:S(2)}) collective-permute-start(bf16[15,512]{1,0:T(8,128)(2,1)S(1)} %get-tuple-element.71), channel_id=1, source_target_pairs={{0,4},{4,8},{8,12},{12,16},{16,20},{20,24},{24,28},{28,32},{32,36}... | collective-permute-start | bytes 46088 | tf_op jit(solution)/shard_map/ppermute | solution.py:20
  340.9 0.0 collective-permute-done.3
  340.9 0.5 collective-permute-done.2
  341.4 1.3 convolution_convert_fusion
  342.7 0.0 reduce-scatter.8.cloned.1.call-update
  342.7 26.5 %reduce-scatter.8.cloned.1.call-done = bf16[48,256]{1,0:T(8,128)(2,1)} async-done(((bf16[48,1024]{1,0:T(8,128)(2,1)}), bf16[48,256]{1,0:T(8,128)(2,1)}) %reduce-scatter.8.cloned.1.call-update) | async-done | bytes 24592 | tf_op jit(solution)/shard_map/reduce_scatter | solution.py:123
  369.2 1.4 add_convert_fusion
  (128 shorter events, 0.3 us)
Async XLA Ops:
  6.5 334.9 %copy-start = (bf16[2,256,1024]{2,1,0:T(8,128)(2,1)S(1)}, bf16[2,256,1024]{2,1,0:T(8,128)(2,1)}, u32[]{:S(2)}) copy-start(bf16[2,256,1024]{2,1,0:T(8,128)(2,1)} %param.19) | copy-start | bytes 3145732
  6.5 140.1 %all-gather.3.cloned.1.call-start = ((), (), s32[]{:S(2)}) async-start(), calls=%async_computation.3 | async-start | bytes 3170304 | tf_op jit(solution)/shard_map/all_gather | solution.py:59
  7.3 272.1 %all-gather.5.cloned.1.call-start = ((), (), s32[]{:S(2)}) async-start(), calls=%async_computation.4 | async-start | bytes 3170304 | tf_op jit(solution)/shard_map/all_gather | solution.py:60
  8.0 300.5 %reduce-scatter.4.cloned.1.call-start = ((), (), s32[]{:S(2)}) async-start(), calls=%async_computation.5 | async-start | bytes 122880 | tf_op jit(solution)/shard_map/reduce_scatter | solution.py:104
  8.1 2.2 copy-start.8
  10.6 19.6 %copy-start.14 = (f32[31,512]{1,0:T(8,128)S(1)}, f32[31,512]{1,0:T(8,128)}, u32[]{:S(2)}) copy-start(f32[31,512]{1,0:T(8,128)} %param.16) | copy-start | bytes 190468
  10.6 136.1 %copy-start.9 = (bf16[48,256]{1,0:T(8,128)(2,1)S(1)}, bf16[48,256]{1,0:T(8,128)(2,1)}, u32[]{:S(2)}) copy-start(bf16[48,256]{1,0:T(8,128)(2,1)} %param.11) | copy-start | bytes 73732
  11.5 137.4 %copy-start.11 = (bf16[48,1024]{1,0:T(8,128)(2,1)}, bf16[48,1024]{1,0:T(8,128)(2,1)S(1)}, u32[]{:S(2)}) copy-start(bf16[48,1024]{1,0:T(8,128)(2,1)S(1)} %fusion.58) | copy-start | bytes 294916
  24.3 262.7 %collective-permute-start.1 = (bf16[15,512]{1,0:T(8,128)(2,1)}, bf16[15,512]{1,0:T(8,128)(2,1)}, u32[]{:S(2)}, u32[]{:S(2)}) collective-permute-start(bf16[15,512]{1,0:T(8,128)(2,1)} %get-tuple-element.74), channel_id=1, source_target_pairs={{4,0},{8,4},{12,8},{16,12},{20,16},{24,20},{28,24},{32,28},{36,32}... | collective-permute-start | bytes 46088 | tf_op jit(solution)/shard_map/ppermute | solution.py:22
  25.6 261.4 %collective-permute-start = (bf16[15,512]{1,0:T(8,128)(2,1)}, bf16[15,512]{1,0:T(8,128)(2,1)}, u32[]{:S(2)}, u32[]{:S(2)}) collective-permute-start(bf16[15,512]{1,0:T(8,128)(2,1)} %get-tuple-element.73), channel_id=1, source_target_pairs={{0,4},{4,8},{8,12},{12,16},{16,20},{20,24},{24,28},{28,32},{32,36}... | collective-permute-start | bytes 46088 | tf_op jit(solution)/shard_map/ppermute | solution.py:20
  146.7 3.8 %copy-start.2 = (bf16[6144,256]{1,0:T(8,128)(2,1)S(1)}, bf16[6144,256]{1,0:T(8,128)(2,1)}, u32[]{:S(2)}) copy-start(bf16[6144,256]{1,0:T(8,128)(2,1)} %all-gather.3.cloned.1.call-done) | copy-start | bytes 9437188
  149.0 0.6 copy-start.15
  149.0 1.5 copy-start.10
  151.3 0.5 copy-start.16
  153.4 0.5 copy-start.17
  153.4 2.2 copy-start.3
  155.6 1.0 copy-start.5
  155.6 1.0 copy-start.19
  279.3 4.3 %copy-start.1 = (bf16[6144,256]{1,0:T(8,128)(2,1)S(1)}, bf16[6144,256]{1,0:T(8,128)(2,1)}, u32[]{:S(2)}) copy-start(bf16[6144,256]{1,0:T(8,128)(2,1)} %all-gather.5.cloned.1.call-done) | copy-start | bytes 9437188
  281.6 2.0 copy-start.4
  281.6 2.0 copy-start.18
  281.7 2.0 copy-start.21
  283.7 1.3 copy-start.6
  283.7 1.3 copy-start.20
  283.7 1.3 copy-start.22
  284.9 1.0 copy-start.7
  284.9 2.0 copy-start.12
  284.9 2.0 copy-start.23
  285.0 2.0 copy-start.24
  285.0 2.0 copy-start.25
  285.0 2.0 copy-start.26
  285.0 2.0 copy-start.27
  285.0 2.0 copy-start.28
  285.0 2.0 copy-start.29
  285.0 2.0 copy-start.30
  285.0 2.0 copy-start.31
  285.0 2.0 copy-start.32
  285.0 2.0 copy-start.33
  285.1 2.0 copy-start.34
  285.1 2.0 copy-start.35
  285.1 2.0 copy-start.36
  285.1 2.0 copy-start.37
  285.1 2.0 copy-start.38
  285.1 2.0 copy-start.39
  285.1 2.0 copy-start.40
  285.1 2.0 copy-start.41
  285.1 2.0 copy-start.42
  285.1 2.0 copy-start.43
  285.2 2.0 copy-start.44
  285.2 2.0 copy-start.45
  285.2 2.0 copy-start.46
  285.2 2.0 copy-start.47
  285.2 2.0 copy-start.48
  285.2 2.0 copy-start.49
  285.2 2.0 copy-start.50
  285.2 2.0 copy-start.51
  286.9 47.6 %reduce-scatter.6.cloned.1.call-start = ((), (), s32[]{:S(2)}) async-start(), calls=%async_computation.6 | async-start | bytes 122880 | tf_op jit(solution)/shard_map/reduce_scatter | solution.py:107
  287.3 3.4 copy-start.13
  290.6 78.6 %reduce-scatter.8.cloned.1.call-start = ((), (), s32[]{:S(2)}) async-start(), calls=%async_computation.7 | async-start | bytes 122880 | tf_op jit(solution)/shard_map/reduce_scatter | solution.py:123
  335.2 5.6 %collective-permute-start.3 = (bf16[15,512]{1,0:T(8,128)(2,1)S(1)}, bf16[15,512]{1,0:T(8,128)(2,1)S(1)}, u32[]{:S(2)}, u32[]{:S(2)}) collective-permute-start(bf16[15,512]{1,0:T(8,128)(2,1)S(1)} %get-tuple-element.72), channel_id=1, source_target_pairs={{4,0},{8,4},{12,8},{16,12},{20,16},{24,20},{28,24},{32,28},{36,32}... | collective-permute-start | bytes 46088 | tf_op jit(solution)/shard_map/ppermute | solution.py:22
  336.5 4.8 %collective-permute-start.2 = (bf16[15,512]{1,0:T(8,128)(2,1)S(1)}, bf16[15,512]{1,0:T(8,128)(2,1)S(1)}, u32[]{:S(2)}, u32[]{:S(2)}) collective-permute-start(bf16[15,512]{1,0:T(8,128)(2,1)S(1)} %get-tuple-element.71), channel_id=1, source_target_pairs={{0,4},{4,8},{8,12},{12,16},{16,20},{20,24},{24,28},{28,32},{32,36}... | collective-permute-start | bytes 46088 | tf_op jit(solution)/shard_map/ppermute | solution.py:20
Sparse Core Ops, SparseCore 0:
  11.7 134.9 all-gather.2
  151.0 128.3 all-gather.4
  287.0 21.4 reduce-scatter.3
  311.4 23.0 reduce-scatter.5
  342.8 26.2 reduce-scatter.7
where the time goes:
time: 378 us; the launch traced here: 377 us
  waiting for transfers between devices  308 us (81%)
  matrix products  16.3 us (4%)
  between operations  14.2 us (4%)
  blocking collectives  11.9 us (3%)
  starting transfers between devices  11.3 us (3%)
  local copies, waits for them, and re-layouts  9.38 us (2%)
  other arithmetic  5.47 us (1%)
    all_gather x1, waiting for transfers between devices, on_device(): lax.all_gather(value_rows, 'seq', axis=0, tiled=True)  122 us
    all_gather x1, waiting for transfers between devices, on_device(): lax.all_gather(key_rows, 'seq', axis=0, tiled=True)  115 us
    reduce_scatter x1, waiting for transfers between devices, on_device(): lax.psum_scatter(merge_part.astype(jnp.bfloat16), 'tp', scatter_dimension...  26.5 us
    reduce_scatter x1, waiting for transfers between devices, on_device(): lax.psum_scatter(cg_part.astype(jnp.bfloat16), 'tp', scatter_dimension=1,...  25.3 us
    reduce_scatter x1, waiting for transfers between devices, on_device(): lax.psum_scatter(att_part.astype(jnp.bfloat16), 'tp', scatter_dimension=1...  17.8 us
    psum x1, blocking collectives, on_device(): lax.psum((jnp.sum(gate_float, -1), jnp.sum(gate_float * gate_float, -1)),...  11.9 us
    ppermute x2, starting transfers between devices, with_halo(): lax.ppermute(tail, axis, [(i, (i + 1) % count) for i in range(ends)])  8.57 us
  transfers between devices with their start and end apart: 9, of which 6 were waited for; matrix products, arithmetic and copies ran while one was open for 6% of the time, Pallas kernels for 0%

commit v1 on v0

v1 whole, which is shorter than its diff:
```python
import functools

import jax
import jax.numpy as jnp
from jax import lax
from jax.experimental import pallas as pl
from jax.experimental.pallas import tpu as pltpu
from jax.sharding import PartitionSpec as P

HEAD = 64
CH = 2048
TAPS = 31
HALO = 16
HEADS_HERE = 4
RING = 8
LOG2E = 1.4426950408889634
LN2 = 0.6931471805599453
F32 = jnp.float32
BF16 = jnp.bfloat16
MESH = pl.DeviceIdType.MESH


def low_lanes(rows):
    return lax.broadcasted_iota(jnp.int32, (rows, 128), 1) < HEAD


def depthwise(pad_ref, taps_ref, column, rows):
    lanes = pl.ds(column, 128)
    total = jnp.zeros((rows, 128), F32)
    for phase in range(8):
        shifted = pad_ref[pl.ds(phase, rows + 24 if phase else rows + 32), lanes]
        for start in range(0, 33, 8):
            j = start + phase - 1
            if 0 <= j < TAPS:
                total = total + taps_ref[pl.ds(j, 1), lanes] * shifted[start : start + rows]
    return total


def kernel(
    seq_size,
    tp_size,
    frames,
    query,
    key,
    value,
    w_out_hbm,
    w_in_hbm,
    w_conv_hbm,
    w_proj_hbm,
    w_blend_hbm,
    w_merge_hbm,
    out,
    w_out,
    w_in,
    w_conv,
    w_proj,
    w_blend,
    w_merge,
    kv_send,
    q_send,
    kv_all,
    kv_ones,
    q_all,
    o_send,
    o_recv,
    gate_half,
    resid_half,
    gate_prev,
    gate_next,
    stat_send,
    stat_recv,
    stat_prev,
    stat_next,
    gate_pad,
    part_send,
    part_recv,
    part_prev,
    part_next,
    blend_pad,
    taps_pad,
    fin_acc,
    fin_send,
    fin_recv,
    weight_sem,
    kv_ss,
    kv_rs,
    ring_ss,
    ring_rs,
    q_ss,
    q_rs,
    o_ss,
    o_rs,
    gate_ss,
    gate_rs,
    stat_ss,
    stat_rs,
    stat_hs,
    stat_hr,
    part_ss,
    part_rs,
    part_hs,
    part_hr,
    fin_ss,
    fin_rs,
):
    rows = query.shape[0]
    wide = rows + 2 * HALO
    seq = lax.axis_index("seq")
    tp = lax.axis_index("tp")
    groups = seq_size // RING
    lane_at = lax.rem(seq, RING)
    group = seq // RING
    head_at = lax.rem(group, HEADS_HERE)
    block = group // HEADS_HERE
    after = lax.rem(seq + 1, seq_size)
    before = lax.rem(seq + seq_size - 1, seq_size)

    def head_peer(i):
        other = lax.rem(head_at + i, HEADS_HERE)
        return other, (block * HEADS_HERE + other) * RING + lane_at

    def group_peer(i):
        other = lax.rem(group + i, groups)
        return other, other * RING + lane_at

    def ring_peer(i):
        other = lax.rem(lane_at + i, RING)
        return group * RING + other

    def tp_peer(i):
        return lax.rem(tp + i, tp_size)

    def send(src, dst, send_sem, recv_sem, to_seq, to_tp):
        return pltpu.make_async_remote_copy(
            src_ref=src,
            dst_ref=dst,
            send_sem=send_sem,
            recv_sem=recv_sem,
            device_id=(to_seq, to_tp),
            device_id_type=MESH,
        )

    weights = [
        pltpu.make_async_copy(src, dst, weight_sem.at[i])
        for i, (src, dst) in enumerate(
            (
                (w_in_hbm, w_in),
                (w_conv_hbm, w_conv),
                (w_proj_hbm, w_proj),
                (w_blend_hbm, w_blend),
                (w_merge_hbm, w_merge),
                (w_out_hbm, w_out),
            )
        )
    ]
    for copy in weights:
        copy.start()

    barrier = pltpu.get_barrier_semaphore()

    def greet(to_seq, to_tp):
        pl.semaphore_signal(barrier, inc=1, device_id=(to_seq, to_tp), device_id_type=MESH)

    @pl.loop(1, groups)
    def _(i):
        greet(group_peer(i)[1], tp)

    @pl.loop(1, RING)
    def _(i):
        greet(ring_peer(i), tp)

    @pl.loop(1, tp_size)
    def _(i):
        greet(seq, tp_peer(i))

    @pl.loop(0, tp_size)
    def _(i):
        greet(after, i)
        greet(before, i)

    low = low_lanes(rows)
    for pair in range(HEADS_HERE // 2):
        lanes = pl.ds(pair * 128, 128)
        k2 = key[:, lanes].astype(F32)
        v2 = value[:, lanes].astype(F32)
        q2 = query[:, lanes].astype(F32)
        kv_send[2 * pair] = jnp.where(low, k2, pltpu.roll(v2, HEAD, 1)).astype(BF16)
        kv_send[2 * pair + 1] = jnp.where(low, pltpu.roll(k2, HEAD, 1), v2).astype(BF16)
        q_send[2 * pair] = jnp.where(low, q2, 0.0).astype(BF16)
        q_send[2 * pair + 1] = jnp.where(low, pltpu.roll(q2, HEAD, 1), 0.0).astype(BF16)
    kv_all[lane_at, head_at] = kv_send[head_at]
    q_all[group] = q_send[head_at]

    pl.semaphore_wait(barrier, (groups - 1) + (RING - 1) + (tp_size - 1) + 2 * tp_size)

    def kv_copy(i):
        other, to = head_peer(i)
        return send(
            kv_send.at[other], kv_all.at[lane_at, head_at], kv_ss.at[i], kv_rs.at[i], to, tp
        )

    def q_copy(i):
        other, to = group_peer(i)
        return send(
            q_send.at[lax.rem(other, HEADS_HERE)],
            q_all.at[group],
            q_ss.at[i],
            q_rs.at[i],
            to,
            tp,
        )

    def ring_copy(i):
        return send(
            kv_all.at[lane_at], kv_all.at[lane_at], ring_ss.at[i], ring_rs.at[i], ring_peer(i), tp
        )

    @pl.loop(1, HEADS_HERE)
    def _(i):
        kv_copy(i).start()

    @pl.loop(1, groups)
    def _(i):
        q_copy(i).start()

    features = frames[...].astype(F32)
    centered = features - jnp.mean(features, -1, keepdims=True)
    variance = jnp.mean(centered * centered, -1, keepdims=True)
    normed = (centered * lax.rsqrt(variance + 1e-05)).astype(BF16)

    @pl.loop(1, HEADS_HERE)
    def _(i):
        kv_copy(i).wait_recv()

    @pl.loop(1, RING)
    def _(i):
        ring_copy(i).start()

    weights[0].wait()

    def hidden_half(half):
        product = jnp.dot(normed, w_in[:, half, :], preferred_element_type=F32)
        return (0.5 * product * (1.0 + lax.erf(product * 0.7071067811865476))).astype(BF16)

    gate = hidden_half(1)
    gate_half[...] = gate
    gate_float = gate.astype(F32)
    sums = jnp.sum(gate_float, -1, keepdims=True)
    squares = jnp.sum(gate_float * gate_float, -1, keepdims=True)
    stat_send[...] = jnp.where(low, sums, squares)

    tail = pl.ds(rows - HALO, HALO)
    head = pl.ds(0, HALO)

    def gate_copies():
        return (
            send(gate_half.at[tail], gate_prev, gate_ss.at[0], gate_rs.at[0], after, tp),
            send(gate_half.at[head], gate_next, gate_ss.at[1], gate_rs.at[1], before, tp),
        )

    def stat_copy(i):
        return send(
            stat_send, stat_recv.at[tp], stat_ss.at[i], stat_rs.at[i], seq, tp_peer(i)
        )

    def stat_halo(i):
        to = tp_peer(i)
        return (
            send(
                stat_send.at[tail], stat_prev.at[tp], stat_hs.at[0, i], stat_hr.at[0, i], after, to
            ),
            send(
                stat_send.at[head], stat_next.at[tp], stat_hs.at[1, i], stat_hr.at[1, i], before, to
            ),
        )

    @pl.loop(1, tp_size)
    def _(i):
        stat_copy(i).start()

    @pl.loop(0, tp_size)
    def _(i):
        for copy in stat_halo(i):
            copy.start()

    for copy in gate_copies():
        copy.start()
    stat_recv[tp] = stat_send[...]

    resid_half[...] = hidden_half(0)

    @pl.loop(1, tp_size)
    def _(i):
        stat_copy(i).wait_recv()

    @pl.loop(0, tp_size)
    def _(i):
        for copy in stat_halo(i):
            copy.wait_recv()

    for copy in gate_copies():
        copy.wait_recv()

    def gate_normed(part, stats, keep):
        total = jnp.sum(stats[...], 0)
        average = total[:, 0:1] / CH
        variance = total[:, HEAD : HEAD + 1] / CH - average * average
        result = (part[...].astype(F32) - average) * lax.rsqrt(variance + 1e-05)
        result = result.astype(BF16).astype(F32)
        return result if keep is None else jnp.where(keep, result, 0.0)

    first, last = seq == 0, seq == seq_size - 1
    gate_pad[pl.ds(0, HALO)] = gate_normed(gate_prev, stat_prev, jnp.logical_not(first))
    gate_pad[pl.ds(HALO, rows)] = gate_normed(gate_half, stat_recv, None)
    gate_pad[pl.ds(HALO + rows, HALO)] = gate_normed(gate_next, stat_next, jnp.logical_not(last))
    weights[1].wait()
    weights[2].wait()
    cg_part = jnp.zeros((rows, w_proj.shape[1]), F32)
    gated = []
    for column in range(0, resid_half.shape[1], 128):
        conv = depthwise(gate_pad, w_conv, column, rows)
        resid = resid_half[:, pl.ds(column, 128)].astype(F32)
        gated.append((resid * conv).astype(BF16))
    cg_part = jnp.dot(jnp.concatenate(gated, 1), w_proj[...], preferred_element_type=F32)

    width = out.shape[1]

    def part_copy(which, i):
        to = tp_peer(i)
        return send(
            part_send.at[which, to],
            part_recv.at[which, tp],
            part_ss.at[which, i],
            part_rs.at[which, i],
            seq,
            to,
        )

    def part_halo(which, i):
        to = tp_peer(i)
        return (
            send(
                part_send.at[which, to, tail],
                part_prev.at[which, tp],
                part_hs.at[which, 0, i],
                part_hr.at[which, 0, i],
                after,
                to,
            ),
            send(
                part_send.at[which, to, head],
                part_next.at[which, tp],
                part_hs.at[which, 1, i],
                part_hr.at[which, 1, i],
                before,
                to,
            ),
        )

    def scatter_part(which, part):
        for i in range(tp_size):
            part_send[which, i] = part[:, i * width : (i + 1) * width].astype(BF16)

        @pl.loop(1, tp_size)
        def _(i):
            part_copy(which, i).start()

        @pl.loop(0, tp_size)
        def _(i):
            for copy in part_halo(which, i):
                copy.start()

        part_recv[which, tp] = part_send[which, tp]

    def merge_part(which):
        @pl.loop(1, tp_size)
        def _(i):
            part_copy(which, i).wait_recv()

        @pl.loop(0, tp_size)
        def _(i):
            for copy in part_halo(which, i):
                copy.wait_recv()

        def joined(ref):
            return jnp.sum(ref[which].astype(F32), 0).astype(BF16).astype(F32)

        own = joined(part_recv)
        blend_pad[pl.ds(0, HALO)] = jnp.where(first, 0.0, joined(part_prev))
        blend_pad[pl.ds(HALO, rows)] = own
        blend_pad[pl.ds(HALO + rows, HALO)] = jnp.where(last, 0.0, joined(part_next))
        taps_pad[...] = w_blend[:, which, :]
        mixture = [
            (own[:, c : c + 128] + depthwise(blend_pad, taps_pad, c, rows)).astype(BF16)
            for c in range(0, width, 128)
        ]
        return jnp.dot(jnp.concatenate(mixture, 1), w_merge[which], preferred_element_type=F32)

    scatter_part(1, cg_part)

    @pl.loop(1, groups)
    def _(i):
        q_copy(i).wait_recv()

    @pl.loop(1, RING)
    def _(i):
        ring_copy(i).wait_recv()

    keys = RING * HEADS_HERE * rows
    kv = kv_all[...].reshape(keys, 128)
    kv_ones[...] = jnp.where(low_lanes(keys), jnp.ones((), BF16), kv)

    def o_copy(other):
        return send(
            o_send.at[other], o_recv.at[group], o_ss.at[other], o_rs.at[group], other * RING + lane_at, tp
        )

    per_step = 4

    @pl.loop(0, groups // per_step)
    def _(step):
        count = per_step * rows
        q = q_all[pl.ds(step * per_step, per_step)].reshape(count, 128)
        kv = kv_all[...].reshape(keys, 128)
        scores = lax.dot_general(q, kv, (((1,), (1,)), ((), ())), preferred_element_type=F32)
        peak = jnp.max(scores, -1, keepdims=True)
        weight = jnp.exp2((scores - peak) * (LOG2E * HEAD**-0.5)).astype(BF16)
        mixed = jnp.dot(weight, kv_ones[...], preferred_element_type=F32)
        low_q = low_lanes(count)
        total = jnp.where(low_q, mixed, pltpu.roll(mixed, HEAD, 1))
        level = peak * HEAD**-0.5 + jnp.log(total)
        level_high = level.astype(BF16).astype(F32)
        lane = lax.broadcasted_iota(jnp.int32, (count, 128), 1)
        packed = jnp.where(
            low_q,
            jnp.where(lane < HEAD // 2, level_high, level - level_high),
            mixed / total,
        ).astype(BF16)
        o_send[pl.ds(step * per_step, per_step)] = packed.reshape(per_step, rows, 128)
        for i in range(per_step):
            other = step * per_step + i

            @pl.when(other != group)
            def _():
                o_copy(other).start()

            @pl.when(other == group)
            def _():
                o_recv[other] = o_send[other]

    for i in (3, 4):
        weights[i].wait()
    fin_acc[...] = merge_part(1)
    weights[5].wait()

    def o_arrival(other):
        return send(
            o_send.at[other], o_recv.at[other], o_ss.at[other], o_rs.at[other], other * RING + lane_at, tp
        )

    @pl.loop(1, groups)
    def _(i):
        o_arrival(group_peer(i)[0]).wait_recv()

    heads = []
    for h in range(HEADS_HERE):
        pieces = [
            o_recv[b * HEADS_HERE + h].astype(F32) for b in range(groups // HEADS_HERE)
        ]
        levels = [p[:, 0:1] + p[:, HEAD // 2 : HEAD // 2 + 1] for p in pieces]
        peak = functools.reduce(jnp.maximum, levels)
        shares = [jnp.exp(level - peak) for level in levels]
        whole = functools.reduce(jnp.add, shares)
        mixed = functools.reduce(jnp.add, [s * p for s, p in zip(shares, pieces)])
        heads.append(mixed / whole)
    attended = jnp.concatenate(
        [
            jnp.where(low, pltpu.roll(heads[2 * pair], HEAD, 1), heads[2 * pair + 1]).astype(BF16)
            for pair in range(HEADS_HERE // 2)
        ],
        1,
    )
    scatter_part(0, jnp.dot(attended, w_out[...], preferred_element_type=F32))
    merged = fin_acc[...] + merge_part(0)

    def fin_copy(i):
        to = tp_peer(i)
        return send(fin_send.at[to], fin_recv.at[tp], fin_ss.at[i], fin_rs.at[i], seq, to)

    for i in range(tp_size):
        fin_send[i] = merged[:, i * width : (i + 1) * width].astype(BF16)

    @pl.loop(1, tp_size)
    def _(i):
        fin_copy(i).start()

    fin_recv[tp] = fin_send[tp]

    @pl.loop(1, tp_size)
    def _(i):
        fin_copy(i).wait_recv()

    own = frames[:, pl.ds(pl.multiple_of(tp * width, width), width)].astype(F32)
    out[...] = (own + jnp.sum(fin_recv[...].astype(F32), 0)).astype(BF16)

    @pl.loop(1, HEADS_HERE)
    def _(i):
        kv_copy(i).wait_send()

    @pl.loop(1, groups)
    def _(i):
        q_copy(i).wait_send()
        o_arrival(group_peer(i)[0]).wait_send()

    @pl.loop(1, RING)
    def _(i):
        ring_copy(i).wait_send()

    for copy in gate_copies():
        copy.wait_send()

    @pl.loop(1, tp_size)
    def _(i):
        stat_copy(i).wait_send()
        part_copy(0, i).wait_send()
        part_copy(1, i).wait_send()
        fin_copy(i).wait_send()

    @pl.loop(0, tp_size)
    def _(i):
        for copy in stat_halo(i) + part_halo(0, i) + part_halo(1, i):
            copy.wait_send()


def solution(mesh):
    seq_size, tp_size = mesh.shape["seq"], mesh.shape["tp"]

    def on_device(*args):
        frames, query, key, value, w_out, w_in, w_conv, w_proj, w_blend, w_merge = args
        rows, width = query.shape
        features = frames.shape[1]
        units = w_in.shape[2]
        groups = seq_size // RING
        wide = rows + 2 * HALO
        dma = pltpu.SemaphoreType.DMA
        vmem = pltpu.VMEM
        return pl.pallas_call(
            functools.partial(kernel, seq_size, tp_size),
            out_shape=jax.ShapeDtypeStruct((rows, width), BF16),
            in_specs=[pl.BlockSpec(memory_space=pltpu.VMEM)] * 4
            + [pl.BlockSpec(memory_space=pl.ANY)] * 6,
            out_specs=pl.BlockSpec(memory_space=pltpu.VMEM),
            scratch_shapes=[
                vmem(w_out.shape, BF16),
                vmem(w_in.shape, BF16),
                vmem(w_conv.shape, F32),
                vmem(w_proj.shape, BF16),
                vmem(w_blend.shape, F32),
                vmem(w_merge.shape, BF16),
                vmem((HEADS_HERE, rows, 128), BF16),
                vmem((HEADS_HERE, rows, 128), BF16),
                vmem((RING, HEADS_HERE, rows, 128), BF16),
                vmem((RING * HEADS_HERE * rows, 128), BF16),
                vmem((groups, rows, 128), BF16),
                vmem((groups, rows, 128), BF16),
                vmem((groups, rows, 128), BF16),
                vmem((rows, units), BF16),
                vmem((rows, units), BF16),
                vmem((HALO, units), BF16),
                vmem((HALO, units), BF16),
                vmem((rows, 128), F32),
                vmem((tp_size, rows, 128), F32),
                vmem((tp_size, HALO, 128), F32),
                vmem((tp_size, HALO, 128), F32),
                vmem((wide, units), F32),
                vmem((2, tp_size, rows, width), BF16),
                vmem((2, tp_size, rows, width), BF16),
                vmem((2, tp_size, HALO, width), BF16),
                vmem((2, tp_size, HALO, width), BF16),
                vmem((wide, width), F32),
                vmem((TAPS, width), F32),
                vmem((rows, features), F32),
                vmem((tp_size, rows, width), BF16),
                vmem((tp_size, rows, width), BF16),
                dma((6,)),
                dma((HEADS_HERE,)),
                dma((HEADS_HERE,)),
                dma((RING,)),
                dma((RING,)),
                dma((groups,)),
                dma((groups,)),
                dma((groups,)),
                dma((groups,)),
                dma((2,)),
                dma((2,)),
                dma((tp_size,)),
                dma((tp_size,)),
                dma((2, tp_size)),
                dma((2, tp_size)),
                dma((2, tp_size)),
                dma((2, tp_size)),
                dma((2, 2, tp_size)),
                dma((2, 2, tp_size)),
                dma((tp_size,)),
                dma((tp_size,)),
            ],
            compiler_params=pltpu.CompilerParams(
                collective_id=0,
                has_side_effects=True,
                vmem_limit_bytes=48 * 1024 * 1024,
            ),
        )(*args)

    return jax.shard_map(
        on_device,
        mesh=mesh,
        in_specs=(
            P("seq", None),
            P("seq", "tp"),
            P("seq", "tp"),
            P("seq", "tp"),
            P("tp", None),
            P(None, None, "tp"),
            P(None, "tp"),
            P("tp", None),
            P(None, None, "tp"),
            P(None, "tp", None),
        ),
        out_specs=P("seq", "tp"),
        check_vma=False,
    )
```

time: 378 us -> 65.9 us (0.17)
  waiting for transfers between devices: 308 us -> 0 us
  Pallas kernels: 0 us -> 54.9 us
  matrix products: 16.3 us -> 0 us
  between operations: 14.2 us -> 0.02 us
  blocking collectives: 11.9 us -> 0 us
  starting transfers between devices: 11.3 us -> 0 us
  other arithmetic: 5.47 us -> 0 us
    all_gather x2 -> x0, waiting for transfers between devices: 237 us -> none  [the longest x1 122 us: on_device(): lax.all_gather(value_rows, 'seq', axis=0, tiled=True)]
    reduce_scatter x3 -> x0, waiting for transfers between devices: 69.5 us -> none  [the longest x1 26.5 us: on_device(): lax.psum_scatter(merge_part.astype(jnp.bfloat16), 'tp', scatter_dimension...]
    pallas_call x0 -> x1, Pallas kernels: none -> 54.9 us  [on_device(): pl.pallas_call(functools.partial(kernel, seq_size, tp_size), out_shape=ja...]
    dot_general x12 -> x0, matrix products: 16.3 us -> none  [the longest x4 5.39 us: on_device(): jnp.dot(weights, value_whole[:, head_start:head_start + HEAD], preferred_...]
    psum x1 -> x0, blocking collectives: 11.9 us -> none  [on_device(): lax.psum((jnp.sum(gate_float, -1), jnp.sum(gate_float * gate_float, -1)),...]
    ppermute x4 -> x0, starting transfers between devices: 11.1 us -> none  [the longest x2 8.57 us: with_halo(): lax.ppermute(tail, axis, [(i, (i + 1) % count) for i in range(ends)])]
    reduce_sum x7 -> x0, other arithmetic: 4 us -> none  [the longest x4 3.57 us: on_device(): prob_total = jnp.sum(exp_scores, -1, keepdims=True)]
    unnamed x139 -> x21, local copies, waits for them, and re-layouts: 6.68 us -> 10.5 us
  transfers between devices with their start and end apart: 9 -> 0, of which waited for: 6 -> 0; matrix products, arithmetic and copies ran while one was open for 6% -> 0% of each run, Pallas kernels for 0% -> 0%
where the time goes in v1:
time: 65.9 us; the launch traced here: 65.3 us
  Pallas kernels  54.9 us (83%)
  local copies, waits for them, and re-layouts  10.5 us (16%)
    pallas_call x1, Pallas kernels, on_device(): pl.pallas_call(functools.partial(kernel, seq_size, tp_size), out_shape=ja...  54.9 us
    unnamed x21, local copies, waits for them, and re-layouts  10.5 us

profile of v1, /device:TPU:1, one launch (start us, length us, event | category | flops | bytes accessed | tf_op | source)
XLA Modules:
  0.0 65.3 jit_solution(12138030380356604121)
XLA Ops:
  0.0 0.0 copy-start
  0.0 1.6 %copy-done = bf16[1024,2,512]{2,1,0:T(2,128)(2,1)S(1)} copy-done((bf16[1024,2,512]{2,1,0:T(2,128)(2,1)S(1)}, bf16[1024,2,512]{2,1,0:T(2,128)(2,1)}, u32[]{:S(2)}) %copy-start) | copy-done | bytes 2097176
  1.6 0.0 copy-start.1
  1.6 1.2 %copy-done.1 = bf16[512,1024]{1,0:T(8,128)(2,1)S(1)} copy-done((bf16[512,1024]{1,0:T(8,128)(2,1)S(1)}, bf16[512,1024]{1,0:T(8,128)(2,1)}, u32[]{:S(2)}) %copy-start.1) | copy-done | bytes 1048600
  2.8 0.0 copy-start.2
  2.8 1.2 %copy-done.2 = bf16[2,256,1024]{2,1,0:T(8,128)(2,1)S(1)} copy-done((bf16[2,256,1024]{2,1,0:T(8,128)(2,1)S(1)}, bf16[2,256,1024]{2,1,0:T(8,128)(2,1)}, u32[]{:S(2)}) %copy-start.2) | copy-done | bytes 1048600
  4.0 0.0 copy-start.3
  4.0 1.0 %copy-done.3 = bf16[256,1024]{1,0:T(8,128)(2,1)S(1)} copy-done((bf16[256,1024]{1,0:T(8,128)(2,1)S(1)}, bf16[256,1024]{1,0:T(8,128)(2,1)}, u32[]{:S(2)}) %copy-start.3) | copy-done | bytes 524312
  5.1 0.0 copy-start.4
  5.1 0.9 %copy-done.4 = bf16[48,1024]{1,0:T(8,128)(2,1)S(1)} copy-done((bf16[48,1024]{1,0:T(8,128)(2,1)S(1)}, bf16[48,1024]{1,0:T(8,128)(2,1)}, u32[]{:S(2)}) %copy-start.4) | copy-done | bytes 98328
  6.0 0.0 copy-start.5
  6.0 0.8 %copy-done.5 = f32[31,512]{1,0:T(8,128)S(1)} copy-done((f32[31,512]{1,0:T(8,128)S(1)}, f32[31,512]{1,0:T(8,128)}, u32[]{:S(2)}) %copy-start.5) | copy-done | bytes 63512
  6.8 0.0 copy-start.6
  6.8 0.8 %copy-done.6 = f32[31,2,256]{2,1,0:T(2,128)S(1)} copy-done((f32[31,2,256]{2,1,0:T(2,128)S(1)}, f32[31,2,256]{2,1,0:T(2,128)}, u32[]{:S(2)}) %copy-start.6) | copy-done | bytes 63512
  7.7 0.0 copy-start.7
  7.7 0.7 %copy-done.7 = bf16[48,256]{1,0:T(8,128)(2,1)S(1)} copy-done((bf16[48,256]{1,0:T(8,128)(2,1)S(1)}, bf16[48,256]{1,0:T(8,128)(2,1)}, u32[]{:S(2)}) %copy-start.7) | copy-done | bytes 24600
  8.4 0.0 copy-start.8
  8.4 0.7 %copy-done.8 = bf16[48,256]{1,0:T(8,128)(2,1)S(1)} copy-done((bf16[48,256]{1,0:T(8,128)(2,1)S(1)}, bf16[48,256]{1,0:T(8,128)(2,1)}, u32[]{:S(2)}) %copy-start.8) | copy-done | bytes 24600
  9.1 0.0 copy-start.9
  9.1 0.7 %copy-done.9 = bf16[48,256]{1,0:T(8,128)(2,1)S(1)} copy-done((bf16[48,256]{1,0:T(8,128)(2,1)S(1)}, bf16[48,256]{1,0:T(8,128)(2,1)}, u32[]{:S(2)}) %copy-start.9) | copy-done | bytes 24600
  9.9 54.9 %shard_map.100 = bf16[48,256]{1,0:T(8,128)(2,1)S(1)} custom-call(bf16[48,1024]{1,0:T(8,128)(2,1)S(1)} %copy-done.4, bf16[48,256]{1,0:T(8,128)(2,1)S(1)} %copy-done.7, bf16[48,256]{1,0:T(8,128)(2,1)S(1)} %copy-done.8, bf16[48,256]{1,0:T(8,128)(2,1)S(1)} %copy-done.9, bf16[256,1024]{1,0:T(8,128)(2,1)S(1)} %copy-done.3, bf16[1024,2,512]{2,1,0:T(2,128)(2,1)S(1)} %copy-done, ...), custom_call_target="tpu_custom_call" | custom-call | tf_op jit(solution)/shard_map/pallas_call | solution.py:547
  64.7 0.6 copy.12
Async XLA Ops:
  0.0 1.6 %copy-start = (bf16[1024,2,512]{2,1,0:T(2,128)(2,1)S(1)}, bf16[1024,2,512]{2,1,0:T(2,128)(2,1)}, u32[]{:S(2)}) copy-start(bf16[1024,2,512]{2,1,0:T(2,128)(2,1)} %w_in_hbm.1) | copy-start | bytes 6291460
  1.6 1.2 %copy-start.1 = (bf16[512,1024]{1,0:T(8,128)(2,1)S(1)}, bf16[512,1024]{1,0:T(8,128)(2,1)}, u32[]{:S(2)}) copy-start(bf16[512,1024]{1,0:T(8,128)(2,1)} %w_proj_hbm.1) | copy-start | bytes 3145732
  2.8 1.2 %copy-start.2 = (bf16[2,256,1024]{2,1,0:T(8,128)(2,1)S(1)}, bf16[2,256,1024]{2,1,0:T(8,128)(2,1)}, u32[]{:S(2)}) copy-start(bf16[2,256,1024]{2,1,0:T(8,128)(2,1)} %w_merge_hbm.1) | copy-start | bytes 3145732
  4.0 1.0 %copy-start.3 = (bf16[256,1024]{1,0:T(8,128)(2,1)S(1)}, bf16[256,1024]{1,0:T(8,128)(2,1)}, u32[]{:S(2)}) copy-start(bf16[256,1024]{1,0:T(8,128)(2,1)} %w_out_hbm.1) | copy-start | bytes 1572868
  5.1 0.9 %copy-start.4 = (bf16[48,1024]{1,0:T(8,128)(2,1)S(1)}, bf16[48,1024]{1,0:T(8,128)(2,1)}, u32[]{:S(2)}) copy-start(bf16[48,1024]{1,0:T(8,128)(2,1)} %frames.1) | copy-start | bytes 294916
  6.0 0.8 %copy-start.5 = (f32[31,512]{1,0:T(8,128)S(1)}, f32[31,512]{1,0:T(8,128)}, u32[]{:S(2)}) copy-start(f32[31,512]{1,0:T(8,128)} %w_conv_hbm.1) | copy-start | bytes 190468
  6.8 0.8 %copy-start.6 = (f32[31,2,256]{2,1,0:T(2,128)S(1)}, f32[31,2,256]{2,1,0:T(2,128)}, u32[]{:S(2)}) copy-start(f32[31,2,256]{2,1,0:T(2,128)} %w_blend_hbm.1) | copy-start | bytes 190468
  7.7 0.7 %copy-start.7 = (bf16[48,256]{1,0:T(8,128)(2,1)S(1)}, bf16[48,256]{1,0:T(8,128)(2,1)}, u32[]{:S(2)}) copy-start(bf16[48,256]{1,0:T(8,128)(2,1)} %query.1) | copy-start | bytes 73732
  8.4 0.7 %copy-start.8 = (bf16[48,256]{1,0:T(8,128)(2,1)S(1)}, bf16[48,256]{1,0:T(8,128)(2,1)}, u32[]{:S(2)}) copy-start(bf16[48,256]{1,0:T(8,128)(2,1)} %key.1) | copy-start | bytes 73732
  9.1 0.7 %copy-start.9 = (bf16[48,256]{1,0:T(8,128)(2,1)S(1)}, bf16[48,256]{1,0:T(8,128)(2,1)}, u32[]{:S(2)}) copy-start(bf16[48,256]{1,0:T(8,128)(2,1)} %value.1) | copy-start | bytes 73732

commit v2 on v1

--- a/solution.py
+++ b/solution.py
@@ -39,10 +39,10 @@
 def kernel(
     seq_size,
     tp_size,
-    frames,
-    query,
-    key,
-    value,
+    frames_hbm,
+    query_hbm,
+    key_hbm,
+    value_hbm,
     w_out_hbm,
     w_in_hbm,
     w_conv_hbm,
@@ -50,6 +50,10 @@
     w_blend_hbm,
     w_merge_hbm,
     out,
+    frames,
+    query,
+    key,
+    value,
     w_out,
     w_in,
     w_conv,
@@ -81,6 +85,7 @@
     fin_acc,
     fin_send,
     fin_recv,
+    near_sem,
     weight_sem,
     kv_ss,
     kv_rs,
@@ -140,6 +145,17 @@
             device_id_type=MESH,
         )
 
+    near = [
+        pltpu.make_async_copy(src, dst, near_sem.at[i])
+        for i, (src, dst) in enumerate(
+            (
+                (key_hbm, key),
+                (value_hbm, value),
+                (query_hbm, query),
+                (frames_hbm, frames),
+            )
+        )
+    ]
     weights = [
         pltpu.make_async_copy(src, dst, weight_sem.at[i])
         for i, (src, dst) in enumerate(
@@ -153,7 +169,7 @@
             )
         )
     ]
-    for copy in weights:
+    for copy in near + weights:
         copy.start()
 
     barrier = pltpu.get_barrier_semaphore()
@@ -178,6 +194,8 @@
         greet(after, i)
         greet(before, i)
 
+    for copy in near[:3]:
+        copy.wait()
     low = low_lanes(rows)
     for pair in range(HEADS_HERE // 2):
         lanes = pl.ds(pair * 128, 128)
@@ -223,6 +241,7 @@
     def _(i):
         q_copy(i).start()
 
+    near[3].wait()
     features = frames[...].astype(F32)
     centered = features - jnp.mean(features, -1, keepdims=True)
     variance = jnp.mean(centered * centered, -1, keepdims=True)
@@ -547,10 +566,13 @@
         return pl.pallas_call(
             functools.partial(kernel, seq_size, tp_size),
             out_shape=jax.ShapeDtypeStruct((rows, width), BF16),
-            in_specs=[pl.BlockSpec(memory_space=pltpu.VMEM)] * 4
-            + [pl.BlockSpec(memory_space=pl.ANY)] * 6,
+            in_specs=[pl.BlockSpec(memory_space=pltpu.HBM)] * 10,
             out_specs=pl.BlockSpec(memory_space=pltpu.VMEM),
             scratch_shapes=[
+                vmem(frames.shape, BF16),
+                vmem(query.shape, BF16),
+                vmem(key.shape, BF16),
+                vmem(value.shape, BF16),
                 vmem(w_out.shape, BF16),
                 vmem(w_in.shape, BF16),
                 vmem(w_conv.shape, F32),
@@ -582,6 +604,7 @@
                 vmem((rows, features), F32),
                 vmem((tp_size, rows, width), BF16),
                 vmem((tp_size, rows, width), BF16),
+                dma((4,)),
                 dma((6,)),
                 dma((HEADS_HERE,)),
                 dma((HEADS_HERE,)),
@@ -607,7 +630,7 @@
             compiler_params=pltpu.CompilerParams(
                 collective_id=0,
                 has_side_effects=True,
-                vmem_limit_bytes=48 * 1024 * 1024,
+                vmem_limit_bytes=63 * 1024 * 1024,
             ),
         )(*args)
 

time: 65.9 us -> 56.5 us (0.86)
  local copies, waits for them, and re-layouts: 10.5 us -> 1.35 us
    unnamed x21 -> x1, local copies, waits for them, and re-layouts: 10.5 us -> 1.35 us
where the time goes in v2:
time: 56.5 us; the launch traced here: 56.4 us
  Pallas kernels  55 us (97%)
  local copies, waits for them, and re-layouts  1.35 us (2%)
    pallas_call x1, Pallas kernels, on_device(): pl.pallas_call(functools.partial(kernel, seq_size, tp_size), out_shape=ja...  55 us
    unnamed x1, local copies, waits for them, and re-layouts  1.35 us

profile of v2, /device:TPU:1, one launch (start us, length us, event | category | flops | bytes accessed | tf_op | source)
XLA Modules:
  0.0 56.4 jit_solution(60897138177600741)
XLA Ops:
  0.0 55.0 %shard_map.100 = bf16[48,256]{1,0:T(8,128)(2,1)} custom-call(bf16[48,1024]{1,0:T(8,128)(2,1)} %frames_hbm.1, bf16[48,256]{1,0:T(8,128)(2,1)} %query_hbm.1, bf16[48,256]{1,0:T(8,128)(2,1)} %key_hbm.1, bf16[48,256]{1,0:T(8,128)(2,1)} %value_hbm.1, bf16[256,1024]{1,0:T(8,128)(2,1)} %w_out_hbm.1, bf16[1024,2,512]{2,1,0:T(2,128)(2,1)} %w_in_hbm.1, ...), custom_call_target="tpu_custom_call" | custom-call | tf_op jit(solution)/shard_map/pallas_call | solution.py:566
  55.0 1.3 %copy.12 = bf16[48,256]{1,0:T(8,128)(2,1)} copy(bf16[48,256]{1,0:T(8,128)(2,1)} %shard_map.100) | data formatting | bytes 49152

commit v3 on v2

--- a/solution.py
+++ b/solution.py
@@ -13,6 +13,7 @@
 HALO = 16
 HEADS_HERE = 4
 RING = 8
+DEPTH = 8
 LOG2E = 1.4426950408889634
 LN2 = 0.6931471805599453
 F32 = jnp.float32
@@ -89,8 +90,6 @@
     weight_sem,
     kv_ss,
     kv_rs,
-    ring_ss,
-    ring_rs,
     q_ss,
     q_rs,
     o_ss,
@@ -112,25 +111,30 @@
     wide = rows + 2 * HALO
     seq = lax.axis_index("seq")
     tp = lax.axis_index("tp")
-    groups = seq_size // RING
-    lane_at = lax.rem(seq, RING)
-    group = seq // RING
+    groups = 2 * DEPTH
+    sides = seq_size // (RING * DEPTH)
+    sources = sides * 2 * RING
+    y_at = lax.rem(seq, RING)
+    z_at = lax.rem(seq // RING, DEPTH)
+    x_at = seq // (RING * DEPTH)
+    group = 2 * z_at + lax.rem(y_at, 2)
     head_at = lax.rem(group, HEADS_HERE)
-    block = group // HEADS_HERE
+    source = (x_at * 2 + lax.rem(z_at, 2)) * RING + y_at
     after = lax.rem(seq + 1, seq_size)
     before = lax.rem(seq + seq_size - 1, seq_size)
 
-    def head_peer(i):
-        other = lax.rem(head_at + i, HEADS_HERE)
-        return other, (block * HEADS_HERE + other) * RING + lane_at
+    def group_seq(other):
+        return (x_at * DEPTH + other // 2) * RING + 2 * (y_at // 2) + lax.rem(other, 2)
 
     def group_peer(i):
         other = lax.rem(group + i, groups)
-        return other, other * RING + lane_at
-
-    def ring_peer(i):
-        other = lax.rem(lane_at + i, RING)
-        return group * RING + other
+        return other, group_seq(other)
+
+    def key_peer(i):
+        y = lax.rem(y_at + lax.rem(i, RING), RING)
+        z_low = lax.rem(z_at + lax.rem(i // RING, 2), 2)
+        x = lax.rem(x_at + i // (2 * RING), sides)
+        return 2 * z_low + lax.rem(y, 2), (x * DEPTH + 2 * (z_at // 2) + z_low) * RING + y
 
     def tp_peer(i):
         return lax.rem(tp + i, tp_size)
@@ -181,9 +185,9 @@
     def _(i):
         greet(group_peer(i)[1], tp)
 
-    @pl.loop(1, RING)
-    def _(i):
-        greet(ring_peer(i), tp)
+    @pl.loop(1, sources)
+    def _(i):
+        greet(key_peer(i)[1], tp)
 
     @pl.loop(1, tp_size)
     def _(i):
@@ -204,18 +208,19 @@
         q2 = query[:, lanes].astype(F32)
         kv_send[2 * pair] = jnp.where(low, k2, pltpu.roll(v2, HEAD, 1)).astype(BF16)
         kv_send[2 * pair + 1] = jnp.where(low, pltpu.roll(k2, HEAD, 1), v2).astype(BF16)
-        q_send[2 * pair] = jnp.where(low, q2, 0.0).astype(BF16)
-        q_send[2 * pair + 1] = jnp.where(low, pltpu.roll(q2, HEAD, 1), 0.0).astype(BF16)
-    kv_all[lane_at, head_at] = kv_send[head_at]
+        for h, q in ((2 * pair, q2), (2 * pair + 1, pltpu.roll(q2, HEAD, 1))):
+            q_send[h, pl.ds(0, HALO)] = jnp.where(
+                low_lanes(HALO), q[:HALO], pltpu.roll(q[2 * HALO :], HEAD, 1)
+            ).astype(BF16)
+            q_send[h, pl.ds(HALO, HALO)] = q[HALO : 2 * HALO].astype(BF16)
+    kv_all[source] = kv_send[head_at]
     q_all[group] = q_send[head_at]
 
-    pl.semaphore_wait(barrier, (groups - 1) + (RING - 1) + (tp_size - 1) + 2 * tp_size)
+    pl.semaphore_wait(barrier, (groups - 1) + (sources - 1) + (tp_size - 1) + 2 * tp_size)
 
     def kv_copy(i):
-        other, to = head_peer(i)
-        return send(
-            kv_send.at[other], kv_all.at[lane_at, head_at], kv_ss.at[i], kv_rs.at[i], to, tp
-        )
+        other, to = key_peer(i)
+        return send(kv_send.at[other], kv_all.at[source], kv_ss.at[i], kv_rs.at[i], to, tp)
 
     def q_copy(i):
         other, to = group_peer(i)
@@ -228,13 +233,10 @@
             tp,
         )
 
-    def ring_copy(i):
-        return send(
-            kv_all.at[lane_at], kv_all.at[lane_at], ring_ss.at[i], ring_rs.at[i], ring_peer(i), tp
-        )
-
-    @pl.loop(1, HEADS_HERE)
-    def _(i):
+    order = sorted(
+        range(1, sources), key=lambda i: -(min(i % RING, RING - i % RING) + 2 * (i // (2 * RING)))
+    )
+    for i in order:
         kv_copy(i).start()
 
     @pl.loop(1, groups)
@@ -247,14 +249,6 @@
     variance = jnp.mean(centered * centered, -1, keepdims=True)
     normed = (centered * lax.rsqrt(variance + 1e-05)).astype(BF16)
 
-    @pl.loop(1, HEADS_HERE)
-    def _(i):
-        kv_copy(i).wait_recv()
-
-    @pl.loop(1, RING)
-    def _(i):
-        ring_copy(i).start()
-
     weights[0].wait()
 
     def hidden_half(half):
@@ -266,7 +260,13 @@
     gate_float = gate.astype(F32)
     sums = jnp.sum(gate_float, -1, keepdims=True)
     squares = jnp.sum(gate_float * gate_float, -1, keepdims=True)
-    stat_send[...] = jnp.where(low, sums, squares)
+    stat_lane = lax.broadcasted_iota(jnp.int32, (8, 128), 1)
+    stats = jnp.zeros((8, 128), F32)
+    for k in range(rows // 8):
+        at = slice(8 * k, 8 * k + 8)
+        stats = jnp.where(stat_lane // 8 == k, sums[at], stats)
+        stats = jnp.where(stat_lane // 8 == 8 + k, squares[at], stats)
+    stat_send[...] = stats
 
     tail = pl.ds(rows - HALO, HALO)
     head = pl.ds(0, HALO)
@@ -285,12 +285,8 @@
     def stat_halo(i):
         to = tp_peer(i)
         return (
-            send(
-                stat_send.at[tail], stat_prev.at[tp], stat_hs.at[0, i], stat_hr.at[0, i], after, to
-            ),
-            send(
-                stat_send.at[head], stat_next.at[tp], stat_hs.at[1, i], stat_hr.at[1, i], before, to
-            ),
+            send(stat_send, stat_prev.at[tp], stat_hs.at[0, i], stat_hr.at[0, i], after, to),
+            send(stat_send, stat_next.at[tp], stat_hs.at[1, i], stat_hr.at[1, i], before, to),
         )
 
     @pl.loop(1, tp_size)
@@ -320,18 +316,19 @@
     for copy in gate_copies():
         copy.wait_recv()
 
-    def gate_normed(part, stats, keep):
-        total = jnp.sum(stats[...], 0)
-        average = total[:, 0:1] / CH
-        variance = total[:, HEAD : HEAD + 1] / CH - average * average
+    def gate_normed(part, stats, blocks, keep):
+        total = jnp.sum(stats[...], 0) / CH
+        average = jnp.concatenate([total[:, 8 * k : 8 * k + 1] for k in blocks], 0)
+        square = jnp.concatenate([total[:, HEAD + 8 * k : HEAD + 8 * k + 1] for k in blocks], 0)
+        variance = square - average * average
         result = (part[...].astype(F32) - average) * lax.rsqrt(variance + 1e-05)
         result = result.astype(BF16).astype(F32)
         return result if keep is None else jnp.where(keep, result, 0.0)
 
     first, last = seq == 0, seq == seq_size - 1
-    gate_pad[pl.ds(0, HALO)] = gate_normed(gate_prev, stat_prev, jnp.logical_not(first))
-    gate_pad[pl.ds(HALO, rows)] = gate_normed(gate_half, stat_recv, None)
-    gate_pad[pl.ds(HALO + rows, HALO)] = gate_normed(gate_next, stat_next, jnp.logical_not(last))
+    gate_pad[pl.ds(0, HALO)] = gate_normed(gate_prev, stat_prev, range(rows // 8 - 2, rows // 8), jnp.logical_not(first))
+    gate_pad[pl.ds(HALO, rows)] = gate_normed(gate_half, stat_recv, range(rows // 8), None)
+    gate_pad[pl.ds(HALO + rows, HALO)] = gate_normed(gate_next, stat_next, range(2), jnp.logical_not(last))
     weights[1].wait()
     weights[2].wait()
     cg_part = jnp.zeros((rows, w_proj.shape[1]), F32)
@@ -421,17 +418,17 @@
     def _(i):
         q_copy(i).wait_recv()
 
-    @pl.loop(1, RING)
-    def _(i):
-        ring_copy(i).wait_recv()
-
-    keys = RING * HEADS_HERE * rows
+    @pl.loop(1, sources)
+    def _(i):
+        kv_copy(i).wait_recv()
+
+    keys = sources * rows
     kv = kv_all[...].reshape(keys, 128)
     kv_ones[...] = jnp.where(low_lanes(keys), jnp.ones((), BF16), kv)
 
     def o_copy(other):
         return send(
-            o_send.at[other], o_recv.at[group], o_ss.at[other], o_rs.at[group], other * RING + lane_at, tp
+            o_send.at[other], o_recv.at[group], o_ss.at[other], o_rs.at[group], group_seq(other), tp
         )
 
     per_step = 4
@@ -439,7 +436,13 @@
     @pl.loop(0, groups // per_step)
     def _(step):
         count = per_step * rows
-        q = q_all[pl.ds(step * per_step, per_step)].reshape(count, 128)
+        pieces = []
+        for i in range(per_step):
+            q = q_all[step * per_step + i]
+            q_end = pltpu.roll(q[:HALO].astype(F32), HEAD, 1).astype(BF16)
+            pieces += [q, q_end]
+        q = jnp.concatenate(pieces, 0)
+        q = jnp.where(low_lanes(count), q, jnp.zeros((), BF16))
         kv = kv_all[...].reshape(keys, 128)
         scores = lax.dot_general(q, kv, (((1,), (1,)), ((), ())), preferred_element_type=F32)
         peak = jnp.max(scores, -1, keepdims=True)
@@ -449,13 +452,22 @@
         total = jnp.where(low_q, mixed, pltpu.roll(mixed, HEAD, 1))
         level = peak * HEAD**-0.5 + jnp.log(total)
         level_high = level.astype(BF16).astype(F32)
-        lane = lax.broadcasted_iota(jnp.int32, (count, 128), 1)
-        packed = jnp.where(
-            low_q,
-            jnp.where(lane < HEAD // 2, level_high, level - level_high),
-            mixed / total,
-        ).astype(BF16)
-        o_send[pl.ds(step * per_step, per_step)] = packed.reshape(per_step, rows, 128)
+        level_low = level - level_high
+        mixed = mixed / total
+        lane = lax.broadcasted_iota(jnp.int32, (HALO, 128), 1)
+        for i in range(per_step):
+            thirds = [slice(i * rows + k * HALO, i * rows + (k + 1) * HALO) for k in range(3)]
+            spare = jnp.zeros((HALO, 128), F32)
+            for k, at in enumerate(thirds):
+                spare = jnp.where(lane // 8 == 2 * k, level_high[at], spare)
+                spare = jnp.where(lane // 8 == 2 * k + 1, level_low[at], spare)
+            o_low = low_lanes(HALO)
+            first_rows = jnp.where(o_low, pltpu.roll(mixed[thirds[2]], HEAD, 1), mixed[thirds[0]])
+            other = step * per_step + i
+            o_send[other, pl.ds(0, HALO)] = first_rows.astype(BF16)
+            o_send[other, pl.ds(HALO, HALO)] = jnp.where(o_low, spare, mixed[thirds[1]]).astype(
+                BF16
+            )
         for i in range(per_step):
             other = step * per_step + i
 
@@ -474,7 +486,7 @@
 
     def o_arrival(other):
         return send(
-            o_send.at[other], o_recv.at[other], o_ss.at[other], o_rs.at[other], other * RING + lane_at, tp
+            o_send.at[other], o_recv.at[other], o_ss.at[other], o_rs.at[other], group_seq(other), tp
         )
 
     @pl.loop(1, groups)
@@ -483,10 +495,20 @@
 
     heads = []
     for h in range(HEADS_HERE):
-        pieces = [
-            o_recv[b * HEADS_HERE + h].astype(F32) for b in range(groups // HEADS_HERE)
-        ]
-        levels = [p[:, 0:1] + p[:, HEAD // 2 : HEAD // 2 + 1] for p in pieces]
+        pieces, levels = [], []
+        for b in range(groups // HEADS_HERE):
+            piece = o_recv[b * HEADS_HERE + h].astype(F32)
+            spare = piece[HALO:]
+            pieces.append(jnp.concatenate([piece, pltpu.roll(piece[:HALO], HEAD, 1)], 0))
+            levels.append(
+                jnp.concatenate(
+                    [
+                        spare[:, 16 * k : 16 * k + 1] + spare[:, 16 * k + 8 : 16 * k + 9]
+                        for k in range(3)
+                    ],
+                    0,
+                )
+            )
         peak = functools.reduce(jnp.maximum, levels)
         shares = [jnp.exp(level - peak) for level in levels]
         whole = functools.reduce(jnp.add, shares)
@@ -522,7 +544,7 @@
     own = frames[:, pl.ds(pl.multiple_of(tp * width, width), width)].astype(F32)
     out[...] = (own + jnp.sum(fin_recv[...].astype(F32), 0)).astype(BF16)
 
-    @pl.loop(1, HEADS_HERE)
+    @pl.loop(1, sources)
     def _(i):
         kv_copy(i).wait_send()
 
@@ -530,10 +552,6 @@
     def _(i):
         q_copy(i).wait_send()
         o_arrival(group_peer(i)[0]).wait_send()
-
-    @pl.loop(1, RING)
-    def _(i):
-        ring_copy(i).wait_send()
 
     for copy in gate_copies():
         copy.wait_send()
@@ -559,7 +577,8 @@
         rows, width = query.shape
         features = frames.shape[1]
         units = w_in.shape[2]
-        groups = seq_size // RING
+        groups = 2 * DEPTH
+        sources = seq_size // DEPTH * 2
         wide = rows + 2 * HALO
         dma = pltpu.SemaphoreType.DMA
         vmem = pltpu.VMEM
@@ -580,20 +599,20 @@
                 vmem(w_blend.shape, F32),
                 vmem(w_merge.shape, BF16),
                 vmem((HEADS_HERE, rows, 128), BF16),
-                vmem((HEADS_HERE, rows, 128), BF16),
-                vmem((RING, HEADS_HERE, rows, 128), BF16),
-                vmem((RING * HEADS_HERE * rows, 128), BF16),
-                vmem((groups, rows, 128), BF16),
-                vmem((groups, rows, 128), BF16),
-                vmem((groups, rows, 128), BF16),
+                vmem((HEADS_HERE, 2 * HALO, 128), BF16),
+                vmem((sources, rows, 128), BF16),
+                vmem((sources * rows, 128), BF16),
+                vmem((groups, 2 * HALO, 128), BF16),
+                vmem((groups, 2 * HALO, 128), BF16),
+                vmem((groups, 2 * HALO, 128), BF16),
                 vmem((rows, units), BF16),
                 vmem((rows, units), BF16),
                 vmem((HALO, units), BF16),
                 vmem((HALO, units), BF16),
-                vmem((rows, 128), F32),
-                vmem((tp_size, rows, 128), F32),
-                vmem((tp_size, HALO, 128), F32),
-                vmem((tp_size, HALO, 128), F32),
+                vmem((8, 128), F32),
+                vmem((tp_size, 8, 128), F32),
+                vmem((tp_size, 8, 128), F32),
+                vmem((tp_size, 8, 128), F32),
                 vmem((wide, units), F32),
                 vmem((2, tp_size, rows, width), BF16),
                 vmem((2, tp_size, rows, width), BF16),
@@ -606,10 +625,8 @@
                 vmem((tp_size, rows, width), BF16),
                 dma((4,)),
                 dma((6,)),
-                dma((HEADS_HERE,)),
-                dma((HEADS_HERE,)),
-                dma((RING,)),
-                dma((RING,)),
+                dma((sources,)),
+                dma((sources,)),
                 dma((groups,)),
                 dma((groups,)),
                 dma((groups,)),

time: 56.5 us -> 53.6 us (0.949)
  Pallas kernels: 55 us -> 52.1 us
    pallas_call x1, Pallas kernels: 55 us -> 52.1 us  [on_device(): pl.pallas_call(functools.partial(kernel, seq_size, tp_size), out_shape=ja...]
where the time goes in v3:
time: 53.6 us; the launch traced here: 53.4 us
  Pallas kernels  52.1 us (97%)
  local copies, waits for them, and re-layouts  1.35 us (3%)
    pallas_call x1, Pallas kernels, on_device(): pl.pallas_call(functools.partial(kernel, seq_size, tp_size), out_shape=ja...  52.1 us
    unnamed x1, local copies, waits for them, and re-layouts  1.35 us

profile of v3, /device:TPU:1, one launch (start us, length us, event | category | flops | bytes accessed | tf_op | source)
XLA Modules:
  0.0 53.4 jit_solution(14403426334844930244)
XLA Ops:
  0.0 52.1 %shard_map.100 = bf16[48,256]{1,0:T(8,128)(2,1)} custom-call(bf16[48,1024]{1,0:T(8,128)(2,1)} %frames_hbm.1, bf16[48,256]{1,0:T(8,128)(2,1)} %query_hbm.1, bf16[48,256]{1,0:T(8,128)(2,1)} %key_hbm.1, bf16[48,256]{1,0:T(8,128)(2,1)} %value_hbm.1, bf16[256,1024]{1,0:T(8,128)(2,1)} %w_out_hbm.1, bf16[1024,2,512]{2,1,0:T(2,128)(2,1)} %w_in_hbm.1, ...), custom_call_target="tpu_custom_call" | custom-call | tf_op jit(solution)/shard_map/pallas_call | solution.py:585
  52.1 1.3 %copy.12 = bf16[48,256]{1,0:T(8,128)(2,1)} copy(bf16[48,256]{1,0:T(8,128)(2,1)} %shard_map.100) | data formatting | bytes 49152

commit v4 on v3

--- a/solution.py
+++ b/solution.py
@@ -90,6 +90,8 @@
     weight_sem,
     kv_ss,
     kv_rs,
+    across_ss,
+    across_rs,
     q_ss,
     q_rs,
     o_ss,
@@ -113,13 +115,14 @@
     tp = lax.axis_index("tp")
     groups = 2 * DEPTH
     sides = seq_size // (RING * DEPTH)
-    sources = sides * 2 * RING
+    nearby = 2 * RING
     y_at = lax.rem(seq, RING)
     z_at = lax.rem(seq // RING, DEPTH)
     x_at = seq // (RING * DEPTH)
     group = 2 * z_at + lax.rem(y_at, 2)
     head_at = lax.rem(group, HEADS_HERE)
-    source = (x_at * 2 + lax.rem(z_at, 2)) * RING + y_at
+    place = lax.rem(z_at, 2) * RING + y_at
+    across = lax.rem(seq + RING * DEPTH, seq_size)
     after = lax.rem(seq + 1, seq_size)
     before = lax.rem(seq + seq_size - 1, seq_size)
 
@@ -132,9 +135,12 @@
 
     def key_peer(i):
         y = lax.rem(y_at + lax.rem(i, RING), RING)
-        z_low = lax.rem(z_at + lax.rem(i // RING, 2), 2)
-        x = lax.rem(x_at + i // (2 * RING), sides)
-        return 2 * z_low + lax.rem(y, 2), (x * DEPTH + 2 * (z_at // 2) + z_low) * RING + y
+        z_low = lax.rem(z_at + i // RING, 2)
+        return 2 * z_low + lax.rem(y, 2), (x_at * DEPTH + 2 * (z_at // 2) + z_low) * RING + y
+
+    def key_place(i):
+        y = lax.rem(y_at + RING - lax.rem(i, RING), RING)
+        return lax.rem(z_at + i // RING, 2) * RING + y
 
     def tp_peer(i):
         return lax.rem(tp + i, tp_size)
@@ -185,9 +191,11 @@
     def _(i):
         greet(group_peer(i)[1], tp)
 
-    @pl.loop(1, sources)
+    @pl.loop(1, nearby)
     def _(i):
         greet(key_peer(i)[1], tp)
+
+    greet(across, tp)
 
     @pl.loop(1, tp_size)
     def _(i):
@@ -213,14 +221,20 @@
                 low_lanes(HALO), q[:HALO], pltpu.roll(q[2 * HALO :], HEAD, 1)
             ).astype(BF16)
             q_send[h, pl.ds(HALO, HALO)] = q[HALO : 2 * HALO].astype(BF16)
-    kv_all[source] = kv_send[head_at]
+    kv_all[x_at * nearby + place] = kv_send[head_at]
     q_all[group] = q_send[head_at]
 
-    pl.semaphore_wait(barrier, (groups - 1) + (sources - 1) + (tp_size - 1) + 2 * tp_size)
+    pl.semaphore_wait(barrier, (groups - 1) + nearby + (tp_size - 1) + 2 * tp_size)
 
     def kv_copy(i):
         other, to = key_peer(i)
-        return send(kv_send.at[other], kv_all.at[source], kv_ss.at[i], kv_rs.at[i], to, tp)
+        return send(
+            kv_send.at[other], kv_all.at[x_at * nearby + place], kv_ss.at[i], kv_rs.at[i], to, tp
+        )
+
+    def across_copy(at):
+        slot = kv_all.at[x_at * nearby + at]
+        return send(slot, slot, across_ss.at[at], across_rs.at[at], across, tp)
 
     def q_copy(i):
         other, to = group_peer(i)
@@ -233,15 +247,15 @@
             tp,
         )
 
-    order = sorted(
-        range(1, sources), key=lambda i: -(min(i % RING, RING - i % RING) + 2 * (i // (2 * RING)))
-    )
-    for i in order:
-        kv_copy(i).start()
-
-    @pl.loop(1, groups)
-    def _(i):
-        q_copy(i).start()
+    def hops(kv, i):
+        if kv:
+            return min(i % RING, RING - i % RING) + i // RING
+        return min(i // 2, DEPTH - i // 2) + i % 2
+
+    order = [(kv, i) for kv in (True, False) for i in range(1, nearby)]
+    for kv, i in sorted(order, key=lambda copy: -hops(*copy)):
+        (kv_copy if kv else q_copy)(i).start()
+    across_copy(place).start()
 
     near[3].wait()
     features = frames[...].astype(F32)
@@ -303,6 +317,10 @@
     stat_recv[tp] = stat_send[...]
 
     resid_half[...] = hidden_half(0)
+
+    for i in sorted(range(1, nearby), key=lambda i: hops(True, i)):
+        kv_copy(i).wait_recv()
+        across_copy(key_place(i)).start()
 
     @pl.loop(1, tp_size)
     def _(i):
@@ -418,11 +436,11 @@
     def _(i):
         q_copy(i).wait_recv()
 
-    @pl.loop(1, sources)
-    def _(i):
-        kv_copy(i).wait_recv()
-
-    keys = sources * rows
+    @pl.loop(0, nearby)
+    def _(i):
+        across_copy(i).wait_recv()
+
+    keys = sides * nearby * rows
     kv = kv_all[...].reshape(keys, 128)
     kv_ones[...] = jnp.where(low_lanes(keys), jnp.ones((), BF16), kv)
 
@@ -544,9 +562,13 @@
     own = frames[:, pl.ds(pl.multiple_of(tp * width, width), width)].astype(F32)
     out[...] = (own + jnp.sum(fin_recv[...].astype(F32), 0)).astype(BF16)
 
-    @pl.loop(1, sources)
+    @pl.loop(1, nearby)
     def _(i):
         kv_copy(i).wait_send()
+
+    @pl.loop(0, nearby)
+    def _(i):
+        across_copy(i).wait_send()
 
     @pl.loop(1, groups)
     def _(i):
@@ -625,8 +647,10 @@
                 vmem((tp_size, rows, width), BF16),
                 dma((4,)),
                 dma((6,)),
-                dma((sources,)),
-                dma((sources,)),
+                dma((2 * RING,)),
+                dma((2 * RING,)),
+                dma((2 * RING,)),
+                dma((2 * RING,)),
                 dma((groups,)),
                 dma((groups,)),
                 dma((groups,)),

time: 53.6 us -> 51.8 us (0.966)
  Pallas kernels: 52.1 us -> 50.3 us
    pallas_call x1, Pallas kernels: 52.1 us -> 50.3 us  [on_device(): pl.pallas_call(functools.partial(kernel, seq_size, tp_size), out_shape=ja...]
where the time goes in v4:
time: 51.8 us; the launch traced here: 51.7 us
  Pallas kernels  50.3 us (97%)
  local copies, waits for them, and re-layouts  1.35 us (3%)
    pallas_call x1, Pallas kernels, on_device(): pl.pallas_call(functools.partial(kernel, seq_size, tp_size), out_shape=ja...  50.3 us
    unnamed x1, local copies, waits for them, and re-layouts  1.35 us

profile of v4, /device:TPU:1, one launch (start us, length us, event | category | flops | bytes accessed | tf_op | source)
XLA Modules:
  0.0 51.7 jit_solution(13617621585595700104)
XLA Ops:
  0.0 50.3 %shard_map.100 = bf16[48,256]{1,0:T(8,128)(2,1)} custom-call(bf16[48,1024]{1,0:T(8,128)(2,1)} %frames_hbm.1, bf16[48,256]{1,0:T(8,128)(2,1)} %query_hbm.1, bf16[48,256]{1,0:T(8,128)(2,1)} %key_hbm.1, bf16[48,256]{1,0:T(8,128)(2,1)} %value_hbm.1, bf16[256,1024]{1,0:T(8,128)(2,1)} %w_out_hbm.1, bf16[1024,2,512]{2,1,0:T(2,128)(2,1)} %w_in_hbm.1, ...), custom_call_target="tpu_custom_call" | custom-call | tf_op jit(solution)/shard_map/pallas_call | solution.py:607
  50.3 1.3 %copy.12 = bf16[48,256]{1,0:T(8,128)(2,1)} copy(bf16[48,256]{1,0:T(8,128)(2,1)} %shard_map.100) | data formatting | bytes 49152

commit v5 on v4

--- a/solution.py
+++ b/solution.py
@@ -91,6 +91,7 @@
     kv_ss,
     kv_rs,
     across_ss,
+    direct_ss,
     across_rs,
     q_ss,
     q_rs,
@@ -143,7 +144,7 @@
         return lax.rem(z_at + i // RING, 2) * RING + y
 
     def tp_peer(i):
-        return lax.rem(tp + i, tp_size)
+        return 2 * lax.rem(tp // 2 + i // 2, tp_size // 2) + lax.rem(tp + i, 2)
 
     def send(src, dst, send_sem, recv_sem, to_seq, to_tp):
         return pltpu.make_async_remote_copy(
@@ -182,6 +183,13 @@
     for copy in near + weights:
         copy.start()
 
+    def hops(i):
+        return min(i % RING, RING - i % RING) + i // RING
+
+    near_first = sorted(range(1, nearby), key=hops)
+    direct = [i for i in range(1, nearby) if i % RING in (0, 1, RING - 1)]
+    relayed = [i for i in near_first if i not in direct]
+
     barrier = pltpu.get_barrier_semaphore()
 
     def greet(to_seq, to_tp):
@@ -196,6 +204,8 @@
         greet(key_peer(i)[1], tp)
 
     greet(across, tp)
+    for i in direct:
+        greet(lax.rem(key_peer(i)[1] + RING * DEPTH, seq_size), tp)
 
     @pl.loop(1, tp_size)
     def _(i):
@@ -224,12 +234,24 @@
     kv_all[x_at * nearby + place] = kv_send[head_at]
     q_all[group] = q_send[head_at]
 
-    pl.semaphore_wait(barrier, (groups - 1) + nearby + (tp_size - 1) + 2 * tp_size)
+    pl.semaphore_wait(barrier, (groups - 1) + nearby + len(direct) + (tp_size - 1) + 2 * tp_size)
 
     def kv_copy(i):
         other, to = key_peer(i)
         return send(
             kv_send.at[other], kv_all.at[x_at * nearby + place], kv_ss.at[i], kv_rs.at[i], to, tp
+        )
+
+    def direct_copy(i):
+        other, to = key_peer(i)
+        to = lax.rem(to + RING * DEPTH, seq_size)
+        return send(
+            kv_send.at[other],
+            kv_all.at[x_at * nearby + place],
+            direct_ss.at[i],
+            across_rs.at[place],
+            to,
+            tp,
         )
 
     def across_copy(at):
@@ -247,15 +269,13 @@
             tp,
         )
 
-    def hops(kv, i):
-        if kv:
-            return min(i % RING, RING - i % RING) + i // RING
-        return min(i // 2, DEPTH - i // 2) + i % 2
-
-    order = [(kv, i) for kv in (True, False) for i in range(1, nearby)]
-    for kv, i in sorted(order, key=lambda copy: -hops(*copy)):
-        (kv_copy if kv else q_copy)(i).start()
+    for i in reversed(relayed):
+        kv_copy(i).start()
     across_copy(place).start()
+    for i in direct:
+        direct_copy(i).start()
+    for i in direct:
+        kv_copy(i).start()
 
     near[3].wait()
     features = frames[...].astype(F32)
@@ -303,24 +323,27 @@
             send(stat_send, stat_next.at[tp], stat_hs.at[1, i], stat_hr.at[1, i], before, to),
         )
 
-    @pl.loop(1, tp_size)
-    def _(i):
-        stat_copy(i).start()
-
-    @pl.loop(0, tp_size)
-    def _(i):
+    for i in reversed(range(tp_size)):
         for copy in stat_halo(i):
             copy.start()
-
     for copy in gate_copies():
         copy.start()
+    for i in reversed(range(1, tp_size)):
+        stat_copy(i).start()
     stat_recv[tp] = stat_send[...]
 
+    def hand_on(chosen):
+        for i in chosen:
+            kv_copy(i).wait_recv()
+            across_copy(key_place(i)).start()
+
+    hand_on(relayed[:4])
+    for i in sorted(range(1, groups), key=lambda i: -min(i // 2, DEPTH - i // 2)):
+        q_copy(i).start()
     resid_half[...] = hidden_half(0)
-
-    for i in sorted(range(1, nearby), key=lambda i: hops(True, i)):
+    hand_on(relayed[4:])
+    for i in direct:
         kv_copy(i).wait_recv()
-        across_copy(key_place(i)).start()
 
     @pl.loop(1, tp_size)
     def _(i):
@@ -395,14 +418,11 @@
         for i in range(tp_size):
             part_send[which, i] = part[:, i * width : (i + 1) * width].astype(BF16)
 
-        @pl.loop(1, tp_size)
-        def _(i):
-            part_copy(which, i).start()
-
-        @pl.loop(0, tp_size)
-        def _(i):
+        for i in reversed(range(tp_size)):
             for copy in part_halo(which, i):
                 copy.start()
+        for i in reversed(range(1, tp_size)):
+            part_copy(which, i).start()
 
         part_recv[which, tp] = part_send[which, tp]
 
@@ -453,10 +473,11 @@
 
     @pl.loop(0, groups // per_step)
     def _(step):
+        start = group + groups + jnp.where(step < 2, 6 + 4 * step, 12 * step - 22)
         count = per_step * rows
         pieces = []
         for i in range(per_step):
-            q = q_all[step * per_step + i]
+            q = q_all[lax.rem(start + i, groups)]
             q_end = pltpu.roll(q[:HALO].astype(F32), HEAD, 1).astype(BF16)
             pieces += [q, q_end]
         q = jnp.concatenate(pieces, 0)
@@ -481,13 +502,13 @@
                 spare = jnp.where(lane // 8 == 2 * k + 1, level_low[at], spare)
             o_low = low_lanes(HALO)
             first_rows = jnp.where(o_low, pltpu.roll(mixed[thirds[2]], HEAD, 1), mixed[thirds[0]])
-            other = step * per_step + i
+            other = lax.rem(start + i, groups)
             o_send[other, pl.ds(0, HALO)] = first_rows.astype(BF16)
             o_send[other, pl.ds(HALO, HALO)] = jnp.where(o_low, spare, mixed[thirds[1]]).astype(
                 BF16
             )
         for i in range(per_step):
-            other = step * per_step + i
+            other = lax.rem(start + i, groups)
 
             @pl.when(other != group)
             def _():
@@ -549,8 +570,7 @@
     for i in range(tp_size):
         fin_send[i] = merged[:, i * width : (i + 1) * width].astype(BF16)
 
-    @pl.loop(1, tp_size)
-    def _(i):
+    for i in reversed(range(1, tp_size)):
         fin_copy(i).start()
 
     fin_recv[tp] = fin_send[tp]
@@ -566,9 +586,11 @@
     def _(i):
         kv_copy(i).wait_send()
 
-    @pl.loop(0, nearby)
-    def _(i):
-        across_copy(i).wait_send()
+    for i in direct:
+        direct_copy(i).wait_send()
+    for i in relayed:
+        across_copy(key_place(i)).wait_send()
+    across_copy(place).wait_send()
 
     @pl.loop(1, groups)
     def _(i):
@@ -651,6 +673,7 @@
                 dma((2 * RING,)),
                 dma((2 * RING,)),
                 dma((2 * RING,)),
+                dma((2 * RING,)),
                 dma((groups,)),
                 dma((groups,)),
                 dma((groups,)),

time: 51.8 us -> 49.6 us (0.958)
  Pallas kernels: 50.3 us -> 48 us
    pallas_call x1, Pallas kernels: 50.3 us -> 48 us  [on_device(): pl.pallas_call(functools.partial(kernel, seq_size, tp_size), out_shape=ja...]
where the time goes in v5:
time: 49.6 us; the launch traced here: 49.4 us
  Pallas kernels  48 us (97%)
  local copies, waits for them, and re-layouts  1.35 us (3%)
    pallas_call x1, Pallas kernels, on_device(): pl.pallas_call(functools.partial(kernel, seq_size, tp_size), out_shape=ja...  48 us
    unnamed x1, local copies, waits for them, and re-layouts  1.35 us

profile of v5, /device:TPU:1, one launch (start us, length us, event | category | flops | bytes accessed | tf_op | source)
XLA Modules:
  0.0 49.4 jit_solution(2387624983553188372)
XLA Ops:
  0.0 48.0 %shard_map.100 = bf16[48,256]{1,0:T(8,128)(2,1)} custom-call(bf16[48,1024]{1,0:T(8,128)(2,1)} %frames_hbm.1, bf16[48,256]{1,0:T(8,128)(2,1)} %query_hbm.1, bf16[48,256]{1,0:T(8,128)(2,1)} %key_hbm.1, bf16[48,256]{1,0:T(8,128)(2,1)} %value_hbm.1, bf16[256,1024]{1,0:T(8,128)(2,1)} %w_out_hbm.1, bf16[1024,2,512]{2,1,0:T(2,128)(2,1)} %w_in_hbm.1, ...), custom_call_target="tpu_custom_call" | custom-call | tf_op jit(solution)/shard_map/pallas_call | solution.py:629
  48.1 1.3 %copy.12 = bf16[48,256]{1,0:T(8,128)(2,1)} copy(bf16[48,256]{1,0:T(8,128)(2,1)} %shard_map.100) | data formatting | bytes 49152

commit v6 on v5

--- a/solution.py
+++ b/solution.py
@@ -180,7 +180,7 @@
             )
         )
     ]
-    for copy in near + weights:
+    for copy in near[:3]:
         copy.start()
 
     def hops(i):
@@ -195,26 +195,20 @@
     def greet(to_seq, to_tp):
         pl.semaphore_signal(barrier, inc=1, device_id=(to_seq, to_tp), device_id_type=MESH)
 
-    @pl.loop(1, groups)
-    def _(i):
-        greet(group_peer(i)[1], tp)
-
-    @pl.loop(1, nearby)
-    def _(i):
-        greet(key_peer(i)[1], tp)
-
-    greet(across, tp)
+    far_groups = sorted(range(1, groups), key=lambda i: -min(i // 2, DEPTH - i // 2))
+    for to_group, to_key in zip(far_groups, reversed(near_first)):
+        greet(group_peer(to_group)[1], tp)
+        greet(key_peer(to_key)[1], tp)
     for i in direct:
         greet(lax.rem(key_peer(i)[1] + RING * DEPTH, seq_size), tp)
-
-    @pl.loop(1, tp_size)
-    def _(i):
-        greet(seq, tp_peer(i))
-
-    @pl.loop(0, tp_size)
-    def _(i):
+    for i in range(tp_size):
         greet(after, i)
         greet(before, i)
+    greet(across, tp)
+    for i in range(1, tp_size):
+        greet(seq, tp_peer(i))
+    for copy in near[3:] + weights:
+        copy.start()
 
     for copy in near[:3]:
         copy.wait()
@@ -340,8 +334,8 @@
     hand_on(relayed[:4])
     for i in sorted(range(1, groups), key=lambda i: -min(i // 2, DEPTH - i // 2)):
         q_copy(i).start()
+    hand_on(relayed[4:])
     resid_half[...] = hidden_half(0)
-    hand_on(relayed[4:])
     for i in direct:
         kv_copy(i).wait_recv()
 
@@ -372,13 +366,11 @@
     gate_pad[pl.ds(HALO + rows, HALO)] = gate_normed(gate_next, stat_next, range(2), jnp.logical_not(last))
     weights[1].wait()
     weights[2].wait()
-    cg_part = jnp.zeros((rows, w_proj.shape[1]), F32)
     gated = []
     for column in range(0, resid_half.shape[1], 128):
         conv = depthwise(gate_pad, w_conv, column, rows)
         resid = resid_half[:, pl.ds(column, 128)].astype(F32)
         gated.append((resid * conv).astype(BF16))
-    cg_part = jnp.dot(jnp.concatenate(gated, 1), w_proj[...], preferred_element_type=F32)
 
     width = out.shape[1]
 
@@ -414,16 +406,18 @@
             ),
         )
 
-    def scatter_part(which, part):
-        for i in range(tp_size):
-            part_send[which, i] = part[:, i * width : (i + 1) * width].astype(BF16)
-
+    def columns_of(to):
+        return pl.ds(pl.multiple_of(to * width, width), width)
+
+    def scatter_part(which, rows_here, weight):
         for i in reversed(range(tp_size)):
+            to = tp_peer(i)
+            piece = jnp.dot(rows_here, weight[:, columns_of(to)], preferred_element_type=F32)
+            part_send[which, to] = piece.astype(BF16)
             for copy in part_halo(which, i):
                 copy.start()
-        for i in reversed(range(1, tp_size)):
-            part_copy(which, i).start()
-
+            if i:
+                part_copy(which, i).start()
         part_recv[which, tp] = part_send[which, tp]
 
     def merge_part(which):
@@ -448,9 +442,9 @@
             (own[:, c : c + 128] + depthwise(blend_pad, taps_pad, c, rows)).astype(BF16)
             for c in range(0, width, 128)
         ]
-        return jnp.dot(jnp.concatenate(mixture, 1), w_merge[which], preferred_element_type=F32)
-
-    scatter_part(1, cg_part)
+        return jnp.concatenate(mixture, 1)
+
+    scatter_part(1, jnp.concatenate(gated, 1), w_proj)
 
     @pl.loop(1, groups)
     def _(i):
@@ -520,8 +514,42 @@
 
     for i in (3, 4):
         weights[i].wait()
-    fin_acc[...] = merge_part(1)
+    fin_acc[...] = jnp.dot(merge_part(1), w_merge[1], preferred_element_type=F32)
     weights[5].wait()
+
+    @pl.loop(1, nearby)
+    def _(i):
+        kv_copy(i).wait_send()
+        q_copy(i).wait_send()
+
+    for i in direct:
+        direct_copy(i).wait_send()
+    for i in relayed:
+        across_copy(key_place(i)).wait_send()
+    across_copy(place).wait_send()
+    for copy in gate_copies():
+        copy.wait_send()
+
+    def sent_part(which):
+        @pl.loop(1, tp_size)
+        def _(i):
+            part_copy(which, i).wait_send()
+
+        @pl.loop(0, tp_size)
+        def _(i):
+            for copy in part_halo(which, i):
+                copy.wait_send()
+
+    @pl.loop(1, tp_size)
+    def _(i):
+        stat_copy(i).wait_send()
+
+    @pl.loop(0, tp_size)
+    def _(i):
+        for copy in stat_halo(i):
+            copy.wait_send()
+
+    sent_part(1)
 
     def o_arrival(other):
         return send(
@@ -560,20 +588,26 @@
         ],
         1,
     )
-    scatter_part(0, jnp.dot(attended, w_out[...], preferred_element_type=F32))
-    merged = fin_acc[...] + merge_part(0)
+    scatter_part(0, attended, w_out)
+    mixture = merge_part(0)
 
     def fin_copy(i):
         to = tp_peer(i)
         return send(fin_send.at[to], fin_recv.at[tp], fin_ss.at[i], fin_rs.at[i], seq, to)
 
-    for i in range(tp_size):
-        fin_send[i] = merged[:, i * width : (i + 1) * width].astype(BF16)
-
-    for i in reversed(range(1, tp_size)):
-        fin_copy(i).start()
-
+    for i in reversed(range(tp_size)):
+        to = tp_peer(i)
+        piece = jnp.dot(mixture, w_merge[0, :, columns_of(to)], preferred_element_type=F32)
+        fin_send[to] = (fin_acc[:, columns_of(to)] + piece).astype(BF16)
+        if i:
+            fin_copy(i).start()
     fin_recv[tp] = fin_send[tp]
+
+    @pl.loop(1, groups)
+    def _(i):
+        o_arrival(group_peer(i)[0]).wait_send()
+
+    sent_part(0)
 
     @pl.loop(1, tp_size)
     def _(i):
@@ -582,35 +616,8 @@
     own = frames[:, pl.ds(pl.multiple_of(tp * width, width), width)].astype(F32)
     out[...] = (own + jnp.sum(fin_recv[...].astype(F32), 0)).astype(BF16)
 
-    @pl.loop(1, nearby)
-    def _(i):
-        kv_copy(i).wait_send()
-
-    for i in direct:
-        direct_copy(i).wait_send()
-    for i in relayed:
-        across_copy(key_place(i)).wait_send()
-    across_copy(place).wait_send()
-
-    @pl.loop(1, groups)
-    def _(i):
-        q_copy(i).wait_send()
-        o_arrival(group_peer(i)[0]).wait_send()
-
-    for copy in gate_copies():
-        copy.wait_send()
-
-    @pl.loop(1, tp_size)
-    def _(i):
-        stat_copy(i).wait_send()
-        part_copy(0, i).wait_send()
-        part_copy(1, i).wait_send()
+    for i in range(1, tp_size):
         fin_copy(i).wait_send()
-
-    @pl.loop(0, tp_size)
-    def _(i):
-        for copy in stat_halo(i) + part_halo(0, i) + part_halo(1, i):
-            copy.wait_send()
 
 
 def solution(mesh):

time: 49.6 us -> 48.5 us (0.978)
  Pallas kernels: 48 us -> 46.9 us
    pallas_call x1, Pallas kernels: 48 us -> 46.9 us  [on_device(): pl.pallas_call(functools.partial(kernel, seq_size, tp_size), out_shape=ja...]
where the time goes in v6:
time: 48.5 us; the launch traced here: 48.3 us
  Pallas kernels  46.9 us (97%)
  local copies, waits for them, and re-layouts  1.35 us (3%)
    pallas_call x1, Pallas kernels, on_device(): pl.pallas_call(functools.partial(kernel, seq_size, tp_size), out_shape=ja...  46.9 us
    unnamed x1, local copies, waits for them, and re-layouts  1.35 us

profile of v6, /device:TPU:1, one launch (start us, length us, event | category | flops | bytes accessed | tf_op | source)
XLA Modules:
  0.0 48.3 jit_solution(12705777507089349977)
XLA Ops:
  0.0 46.9 %shard_map.100 = bf16[48,256]{1,0:T(8,128)(2,1)} custom-call(bf16[48,1024]{1,0:T(8,128)(2,1)} %frames_hbm.1, bf16[48,256]{1,0:T(8,128)(2,1)} %query_hbm.1, bf16[48,256]{1,0:T(8,128)(2,1)} %key_hbm.1, bf16[48,256]{1,0:T(8,128)(2,1)} %value_hbm.1, bf16[256,1024]{1,0:T(8,128)(2,1)} %w_out_hbm.1, bf16[1024,2,512]{2,1,0:T(2,128)(2,1)} %w_in_hbm.1, ...), custom_call_target="tpu_custom_call" | custom-call | tf_op jit(solution)/shard_map/pallas_call | solution.py:636
  46.9 1.3 %copy.12 = bf16[48,256]{1,0:T(8,128)(2,1)} copy(bf16[48,256]{1,0:T(8,128)(2,1)} %shard_map.100) | data formatting | bytes 49152

commit v7 on v6

--- a/solution.py
+++ b/solution.py
@@ -190,6 +190,30 @@
     direct = [i for i in range(1, nearby) if i % RING in (0, 1, RING - 1)]
     relayed = [i for i in near_first if i not in direct]
 
+    first, last = seq == 0, seq == seq_size - 1
+
+    def halo_start(copies):
+        pl.when(jnp.logical_not(last))(copies[0].start)
+        pl.when(jnp.logical_not(first))(copies[1].start)
+
+    def halo_sent(copies):
+        pl.when(jnp.logical_not(last))(copies[0].wait_send)
+        pl.when(jnp.logical_not(first))(copies[1].wait_send)
+
+    def halo_arrived(copies):
+        pl.when(jnp.logical_not(first))(copies[0].wait_recv)
+        pl.when(jnp.logical_not(last))(copies[1].wait_recv)
+
+    @pl.when(first)
+    def _():
+        for ref in (gate_prev, stat_prev, part_prev):
+            ref[...] = jnp.zeros(ref.shape, ref.dtype)
+
+    @pl.when(last)
+    def _():
+        for ref in (gate_next, stat_next, part_next):
+            ref[...] = jnp.zeros(ref.shape, ref.dtype)
+
     barrier = pltpu.get_barrier_semaphore()
 
     def greet(to_seq, to_tp):
@@ -318,10 +342,8 @@
         )
 
     for i in reversed(range(tp_size)):
-        for copy in stat_halo(i):
-            copy.start()
-    for copy in gate_copies():
-        copy.start()
+        halo_start(stat_halo(i))
+    halo_start(gate_copies())
     for i in reversed(range(1, tp_size)):
         stat_copy(i).start()
     stat_recv[tp] = stat_send[...]
@@ -345,11 +367,9 @@
 
     @pl.loop(0, tp_size)
     def _(i):
-        for copy in stat_halo(i):
-            copy.wait_recv()
-
-    for copy in gate_copies():
-        copy.wait_recv()
+        halo_arrived(stat_halo(i))
+
+    halo_arrived(gate_copies())
 
     def gate_normed(part, stats, blocks, keep):
         total = jnp.sum(stats[...], 0) / CH
@@ -360,7 +380,6 @@
         result = result.astype(BF16).astype(F32)
         return result if keep is None else jnp.where(keep, result, 0.0)
 
-    first, last = seq == 0, seq == seq_size - 1
     gate_pad[pl.ds(0, HALO)] = gate_normed(gate_prev, stat_prev, range(rows // 8 - 2, rows // 8), jnp.logical_not(first))
     gate_pad[pl.ds(HALO, rows)] = gate_normed(gate_half, stat_recv, range(rows // 8), None)
     gate_pad[pl.ds(HALO + rows, HALO)] = gate_normed(gate_next, stat_next, range(2), jnp.logical_not(last))
@@ -414,8 +433,7 @@
             to = tp_peer(i)
             piece = jnp.dot(rows_here, weight[:, columns_of(to)], preferred_element_type=F32)
             part_send[which, to] = piece.astype(BF16)
-            for copy in part_halo(which, i):
-                copy.start()
+            halo_start(part_halo(which, i))
             if i:
                 part_copy(which, i).start()
         part_recv[which, tp] = part_send[which, tp]
@@ -427,8 +445,7 @@
 
         @pl.loop(0, tp_size)
         def _(i):
-            for copy in part_halo(which, i):
-                copy.wait_recv()
+            halo_arrived(part_halo(which, i))
 
         def joined(ref):
             return jnp.sum(ref[which].astype(F32), 0).astype(BF16).astype(F32)
@@ -527,8 +544,7 @@
     for i in relayed:
         across_copy(key_place(i)).wait_send()
     across_copy(place).wait_send()
-    for copy in gate_copies():
-        copy.wait_send()
+    halo_sent(gate_copies())
 
     def sent_part(which):
         @pl.loop(1, tp_size)
@@ -537,8 +553,7 @@
 
         @pl.loop(0, tp_size)
         def _(i):
-            for copy in part_halo(which, i):
-                copy.wait_send()
+            halo_sent(part_halo(which, i))
 
     @pl.loop(1, tp_size)
     def _(i):
@@ -546,8 +561,7 @@
 
     @pl.loop(0, tp_size)
     def _(i):
-        for copy in stat_halo(i):
-            copy.wait_send()
+        halo_sent(stat_halo(i))
 
     sent_part(1)
 

time: 48.5 us -> 46.9 us (0.967)
  the two profiles are of different devices: /device:TPU:1 before, /device:TPU:4 now
where the time goes in v7:
time: 46.9 us; the launch traced here: 46.7 us
  Pallas kernels  45.3 us (97%)
  local copies, waits for them, and re-layouts  1.35 us (3%)
    pallas_call x1, Pallas kernels, on_device(): pl.pallas_call(functools.partial(kernel, seq_size, tp_size), out_shape=ja...  45.3 us
    unnamed x1, local copies, waits for them, and re-layouts  1.35 us

profile of v7, /device:TPU:4, one launch (start us, length us, event | category | flops | bytes accessed | tf_op | source)
XLA Modules:
  0.0 46.7 jit_solution(12348038884092578756)
XLA Ops:
  0.0 45.3 %shard_map.100 = bf16[48,256]{1,0:T(8,128)(2,1)} custom-call(bf16[48,1024]{1,0:T(8,128)(2,1)} %frames_hbm.1, bf16[48,256]{1,0:T(8,128)(2,1)} %query_hbm.1, bf16[48,256]{1,0:T(8,128)(2,1)} %key_hbm.1, bf16[48,256]{1,0:T(8,128)(2,1)} %value_hbm.1, bf16[256,1024]{1,0:T(8,128)(2,1)} %w_out_hbm.1, bf16[1024,2,512]{2,1,0:T(2,128)(2,1)} %w_in_hbm.1, ...), custom_call_target="tpu_custom_call" | custom-call | tf_op jit(solution)/shard_map/pallas_call | solution.py:650
  45.3 1.3 %copy.12 = bf16[48,256]{1,0:T(8,128)(2,1)} copy(bf16[48,256]{1,0:T(8,128)(2,1)} %shard_map.100) | data formatting | bytes 49152

commit v8 on v7

--- a/solution.py
+++ b/solution.py
@@ -301,6 +301,9 @@
     variance = jnp.mean(centered * centered, -1, keepdims=True)
     normed = (centered * lax.rsqrt(variance + 1e-05)).astype(BF16)
 
+    for i in sorted(range(1, groups), key=lambda i: -min(i // 2, DEPTH - i // 2)):
+        q_copy(i).start()
+
     weights[0].wait()
 
     def hidden_half(half):
@@ -354,8 +357,6 @@
             across_copy(key_place(i)).start()
 
     hand_on(relayed[:4])
-    for i in sorted(range(1, groups), key=lambda i: -min(i // 2, DEPTH - i // 2)):
-        q_copy(i).start()
     hand_on(relayed[4:])
     resid_half[...] = hidden_half(0)
     for i in direct:
@@ -460,8 +461,6 @@
             for c in range(0, width, 128)
         ]
         return jnp.concatenate(mixture, 1)
-
-    scatter_part(1, jnp.concatenate(gated, 1), w_proj)
 
     @pl.loop(1, groups)
     def _(i):
@@ -529,9 +528,10 @@
             def _():
                 o_recv[other] = o_send[other]
 
+    scatter_part(1, jnp.concatenate(gated, 1), w_proj)
+
     for i in (3, 4):
         weights[i].wait()
-    fin_acc[...] = jnp.dot(merge_part(1), w_merge[1], preferred_element_type=F32)
     weights[5].wait()
 
     @pl.loop(1, nearby)
@@ -562,8 +562,6 @@
     @pl.loop(0, tp_size)
     def _(i):
         halo_sent(stat_halo(i))
-
-    sent_part(1)
 
     def o_arrival(other):
         return send(
@@ -603,6 +601,7 @@
         1,
     )
     scatter_part(0, attended, w_out)
+    fin_acc[...] = jnp.dot(merge_part(1), w_merge[1], preferred_element_type=F32)
     mixture = merge_part(0)
 
     def fin_copy(i):
@@ -622,6 +621,7 @@
         o_arrival(group_peer(i)[0]).wait_send()
 
     sent_part(0)
+    sent_part(1)
 
     @pl.loop(1, tp_size)
     def _(i):

time: 46.9 us -> 45.7 us (0.974)
  the two profiles are of different devices: /device:TPU:4 before, /device:TPU:1 now
where the time goes in v8:
time: 45.7 us; the launch traced here: 45 us
  Pallas kernels  43.7 us (96%)
  local copies, waits for them, and re-layouts  1.35 us (3%)
    pallas_call x1, Pallas kernels, on_device(): pl.pallas_call(functools.partial(kernel, seq_size, tp_size), out_shape=ja...  43.7 us
    unnamed x1, local copies, waits for them, and re-layouts  1.35 us

profile of v8, /device:TPU:1, one launch (start us, length us, event | category | flops | bytes accessed | tf_op | source)
XLA Modules:
  0.0 45.0 jit_solution(4425197222321982224)
XLA Ops:
  0.0 43.7 %shard_map.100 = bf16[48,256]{1,0:T(8,128)(2,1)} custom-call(bf16[48,1024]{1,0:T(8,128)(2,1)} %frames_hbm.1, bf16[48,256]{1,0:T(8,128)(2,1)} %query_hbm.1, bf16[48,256]{1,0:T(8,128)(2,1)} %key_hbm.1, bf16[48,256]{1,0:T(8,128)(2,1)} %value_hbm.1, bf16[256,1024]{1,0:T(8,128)(2,1)} %w_out_hbm.1, bf16[1024,2,512]{2,1,0:T(2,128)(2,1)} %w_in_hbm.1, ...), custom_call_target="tpu_custom_call" | custom-call | tf_op jit(solution)/shard_map/pallas_call | solution.py:650
  43.7 1.3 %copy.12 = bf16[48,256]{1,0:T(8,128)(2,1)} copy(bf16[48,256]{1,0:T(8,128)(2,1)} %shard_map.100) | data formatting | bytes 49152

commit v9 on v8

--- a/solution.py
+++ b/solution.py
@@ -234,23 +234,16 @@
     for copy in near[3:] + weights:
         copy.start()
 
-    for copy in near[:3]:
+    for copy in near[:2]:
         copy.wait()
     low = low_lanes(rows)
     for pair in range(HEADS_HERE // 2):
         lanes = pl.ds(pair * 128, 128)
         k2 = key[:, lanes].astype(F32)
         v2 = value[:, lanes].astype(F32)
-        q2 = query[:, lanes].astype(F32)
         kv_send[2 * pair] = jnp.where(low, k2, pltpu.roll(v2, HEAD, 1)).astype(BF16)
         kv_send[2 * pair + 1] = jnp.where(low, pltpu.roll(k2, HEAD, 1), v2).astype(BF16)
-        for h, q in ((2 * pair, q2), (2 * pair + 1, pltpu.roll(q2, HEAD, 1))):
-            q_send[h, pl.ds(0, HALO)] = jnp.where(
-                low_lanes(HALO), q[:HALO], pltpu.roll(q[2 * HALO :], HEAD, 1)
-            ).astype(BF16)
-            q_send[h, pl.ds(HALO, HALO)] = q[HALO : 2 * HALO].astype(BF16)
     kv_all[x_at * nearby + place] = kv_send[head_at]
-    q_all[group] = q_send[head_at]
 
     pl.semaphore_wait(barrier, (groups - 1) + nearby + len(direct) + (tp_size - 1) + 2 * tp_size)
 
@@ -301,6 +294,15 @@
     variance = jnp.mean(centered * centered, -1, keepdims=True)
     normed = (centered * lax.rsqrt(variance + 1e-05)).astype(BF16)
 
+    near[2].wait()
+    for pair in range(HEADS_HERE // 2):
+        q2 = query[:, pl.ds(pair * 128, 128)].astype(F32)
+        for h, q in ((2 * pair, q2), (2 * pair + 1, pltpu.roll(q2, HEAD, 1))):
+            q_send[h, pl.ds(0, HALO)] = jnp.where(
+                low_lanes(HALO), q[:HALO], pltpu.roll(q[2 * HALO :], HEAD, 1)
+            ).astype(BF16)
+            q_send[h, pl.ds(HALO, HALO)] = q[HALO : 2 * HALO].astype(BF16)
+    q_all[group] = q_send[head_at]
     for i in sorted(range(1, groups), key=lambda i: -min(i // 2, DEPTH - i // 2)):
         q_copy(i).start()
 

time: 45.7 us -> 45.7 us (level)
  no operation moved by 1% of the time
where the time goes in v9:
time: 45.7 us; the launch traced here: 45 us
  Pallas kernels  43.7 us (96%)
  local copies, waits for them, and re-layouts  1.35 us (3%)
    pallas_call x1, Pallas kernels, on_device(): pl.pallas_call(functools.partial(kernel, seq_size, tp_size), out_shape=ja...  43.7 us
    unnamed x1, local copies, waits for them, and re-layouts  1.35 us

profile of v9, /device:TPU:1, one launch (start us, length us, event | category | flops | bytes accessed | tf_op | source)
XLA Modules:
  0.0 45.0 jit_solution(3752961101507241277)
XLA Ops:
  0.0 43.7 %shard_map.100 = bf16[48,256]{1,0:T(8,128)(2,1)} custom-call(bf16[48,1024]{1,0:T(8,128)(2,1)} %frames_hbm.1, bf16[48,256]{1,0:T(8,128)(2,1)} %query_hbm.1, bf16[48,256]{1,0:T(8,128)(2,1)} %key_hbm.1, bf16[48,256]{1,0:T(8,128)(2,1)} %value_hbm.1, bf16[256,1024]{1,0:T(8,128)(2,1)} %w_out_hbm.1, bf16[1024,2,512]{2,1,0:T(2,128)(2,1)} %w_in_hbm.1, ...), custom_call_target="tpu_custom_call" | custom-call | tf_op jit(solution)/shard_map/pallas_call | solution.py:652
  43.7 1.3 %copy.12 = bf16[48,256]{1,0:T(8,128)(2,1)} copy(bf16[48,256]{1,0:T(8,128)(2,1)} %shard_map.100) | data formatting | bytes 49152
